TPU v7x, 512 devices: a whole 4x8x8 slice. The times are simulated.
512 devices in a mesh: grp: 16 (over y, z_lo), col: 32 (over x, z_hi, core).
Axes of the slice: x: 4, y: 8, z: 8 (z_hi: 4, z_lo: 2; z = z_hi * 2 + z_lo), core: 2. Of those that a mesh axis runs over, the one named last changes fastest.
Arguments:
- factors: bfloat16 [2048, 16, 1024], P('col', 'grp'), may hold values from -2 to 2
- occ_levels: float32 [16], replicated, may hold values from -2 to -0.3
- vir_levels: float32 [1024], replicated, may hold values from 0.1 to 15
- slot_orbital: int32 [16], replicated, may hold values from 0 to 15, each once
Outputs:
- amplitudes: bfloat16 [16, 1024, 16384], P(None, 'col', 'grp')
- pair_energy: float32 [16, 16], replicated
Inputs may be any that keep to these rules, and one draw needn't show every extreme that they name: `slot_orbital`: each slot holds a different orbital.
All inputs are finite; a program needn't handle non-finite values.
Results may differ from a plain program's by a relative error of at most 0.001.
Values may be sent and summed in bfloat16 or wider, within the bound.
No kernel may reach another device: no remote copies, remote signals or barrier semaphores. Data moves between devices by JAX's collectives and lax.ppermute only.
A program may use at most 64 MiB of HBM per device.

v0:
```python
import jax
import jax.numpy as jnp
from jax import lax
from jax.sharding import PartitionSpec as P


def from_root(value, axis, source):
    kept = jnp.where(lax.axis_index(axis) == source, value, 0).astype(value.dtype)
    return lax.psum(kept, axis)


def per_device(factors, occ_levels, vir_levels, slot_orbital):
    own_count = factors.shape[1]
    vir_count = factors.shape[2]
    col_count = lax.axis_size("col")
    grp_count = lax.axis_size("grp")
    width_first = vir_count // col_count
    width_second = vir_count // grp_count
    col_ratio = col_count // grp_count
    orbitals = own_count * grp_count
    group_index = lax.axis_index("grp")
    column_index = lax.axis_index("col")
    contract = (((1,), (1,)), ((), ()))
    reordered = jnp.transpose(factors, (1, 2, 0))
    gathered = lax.all_gather(reordered, "grp", axis=0, tiled=True)
    first_side = lax.all_to_all(gathered, "col", split_axis=1, concat_axis=2, tiled=True)
    aux_count = first_side.shape[2]
    first_flat = first_side.reshape(orbitals * width_first, aux_count)
    blocks = []
    for offset in range(col_ratio):
        owner_index = group_index * col_ratio + offset
        partner = from_root(first_side, "col", owner_index)
        product = lax.dot_general(
            first_flat,
            partner.reshape(orbitals * width_first, aux_count),
            contract,
            preferred_element_type=jnp.float32,
        )
        blocks.append(product.reshape(orbitals, width_first, orbitals, width_first))
    integrals = jnp.concatenate(blocks, axis=3)
    selector = slot_orbital[:, None] == jnp.arange(orbitals, dtype=jnp.int32)[None, :]
    occ_energy = jnp.sum(jnp.where(selector, occ_levels[None, :], 0.0), axis=1)
    vir_first = lax.dynamic_slice_in_dim(vir_levels, column_index * width_first, width_first)
    vir_second = lax.dynamic_slice_in_dim(vir_levels, group_index * width_second, width_second)
    occ_pair = occ_energy[:, None, None, None] + occ_energy[None, None, :, None]
    denominator = occ_pair - vir_first[None, :, None, None] - vir_second[None, None, None, :]
    amp_local = (integrals / denominator).astype(jnp.bfloat16)
    amplitudes = jnp.transpose(amp_local, (0, 1, 3, 2)).reshape(
        orbitals, width_first, width_second * orbitals
    )
    swapped = jnp.transpose(integrals, (2, 1, 0, 3))
    pair_part = jnp.sum(integrals * (2.0 * integrals - swapped) / denominator, axis=(1, 3))
    summed = lax.psum(pair_part, ("grp", "col"))
    return (amplitudes, summed / (vir_count * vir_count))


def solution(mesh):
    placed = (P("col", "grp", None), P(), P(), P())
    return jax.shard_map(
        per_device,
        mesh=mesh,
        in_specs=placed,
        out_specs=(P(None, "col", "grp"), P()),
        check_vma=False,
    )
```

profile of v0, /device:TPU:1, one launch (start us, length us, event | category | flops | bytes accessed | tf_op | source)
XLA Modules:
  0.0 651.6 jit_solution(10395145013656813057)
XLA Ops:
  7.9 74.2 %all-gather.2.cloned.1.call-done = bf16[16,1024,64]{1,2,0:T(8,128)(2,1)} async-done(((bf16[1,1024,64]{1,2,0:T(8,128)(2,1)}), bf16[16,1024,64]{1,2,0:T(8,128)(2,1)}) %all-gather.2.cloned.1.call-update) | async-done | bytes 2097168 | tf_op jit(solution)/shard_map/all_gather | solution.py:25
  82.1 6.2 copy.45
  88.3 7.9 %reshape.80 = bf16[32,2,16384]{2,1,0:T(2,128)(2,1)} reshape(bf16[1024,16,64]{2,1,0:T(8,128)(2,1)} %bitcast.40) | data formatting | bytes 4194304
  96.2 19.1 %all-to-all-start = ((bf16[32,2,16384]{2,1,0:T(2,128)(2,1)}), bf16[32,2,16384]{2,1,0:T(2,128)(2,1)S(1)}, u32[]{:S(2)}, u32[]{:S(2)}) async-start(bf16[32,2,16384]{2,1,0:T(2,128)(2,1)} %reshape.80), calls=%async_computation | async-start | bytes 4194304 | tf_op jit(solution)/shard_map/all_to_all | solution.py:26
  115.6 51.6 %all-to-all-done = bf16[32,2,16384]{2,1,0:T(2,128)(2,1)S(1)} async-done(((bf16[32,2,16384]{2,1,0:T(2,128)(2,1)}), bf16[32,2,16384]{2,1,0:T(2,128)(2,1)S(1)}, u32[]{:S(2)}, u32[]{:S(2)}) %all-to-all-start) | async-done | bytes 2097184 | tf_op jit(solution)/shard_map/all_to_all | solution.py:26
  167.1 4.0 reshape.81
  171.1 3.3 copy.46
  176.9 3.7 copy.47
  180.6 6.7 %reshape.70 = bf16[512,2048]{1,0:T(8,128)(2,1)} reshape(bf16[16,32,32,64]{3,2,1,0:T(8,128)(2,1)} %copy.47) | data formatting | bytes 4194304 | tf_op jit(solution)/shard_map/reshape | solution.py:35
  187.3 5.9 copy.50
  193.2 6.8 %reshape.73 = bf16[512,2048]{1,0:T(8,128)(2,1)} reshape(bf16[16,32,32,64]{3,2,1,0:T(8,128)(2,1)} %copy.50) | data formatting | bytes 4194304 | tf_op jit(solution)/shard_map/reshape | solution.py:35
  202.0 6.9 %copy.48 = bf16[16,32,32,64]{3,2,1,0:T(8,128)(2,1)} copy(bf16[16,32,32,64]{3,0,1,2:T(8,128)(2,1)} %bitcast.37) | data formatting | bytes 4194304 | tf_op jit(solution)/shard_map/all_to_all | solution.py:26
  208.8 5.8 reshape.71
  214.6 284.0 %all-reduce.3.cloned.1.call-done = (bf16[512,2048]{1,0:T(8,128)(2,1)}, bf16[512,2048]{1,0:T(8,128)(2,1)}) async-done(((bf16[512,2048]{1,0:T(8,128)(2,1)}, bf16[512,2048]{1,0:T(8,128)(2,1)}), (bf16[512,2048]{1,0:T(8,128)(2,1)}, bf16[512,2048]{1,0:T(8,128)(2,1)})) %all-reduce.3.cloned.1.call-update) | async-done | bytes 4194320 | tf_op jit(solution)/shard_map/psum | solution.py:9
  498.6 2.9 convolution_bitcast_fusion.1
  504.0 6.0 copy.52
  510.0 2.9 convolution_bitcast_fusion
  515.4 6.0 copy.53
  521.4 4.6 broadcast_multiply_fusion
  526.0 6.5 fusion.3
  532.5 2.9 fusion.4
  535.4 4.2 copy.55
  539.6 4.6 copy.59
  544.1 100.0 %psum.23 = f32[16,16]{1,0:T(8,128)S(1)} all-reduce(f32[16,16]{1,0:T(8,128)S(1)} %get-tuple-element.18), channel_id=1, replica_groups=mesh['grp'=16,'col'=32] {'grp','col'}, use_global_device_ids=true, to_apply=%region_4.5 | all-reduce | flops 256 | bytes 2048 | tf_op jit(solution)/shard_map/psum | solution.py:53
  (17 shorter events, 11.0 us)
Async XLA Ops:
  7.2 75.0 %all-gather.2.cloned.1.call-start = ((), (), s32[]{:S(2)}) async-start(), calls=%async_computation.1 | async-start | bytes 2228224 | tf_op jit(solution)/shard_map/all_gather | solution.py:25
  96.2 71.0 %all-to-all-start = ((bf16[32,2,16384]{2,1,0:T(2,128)(2,1)}), bf16[32,2,16384]{2,1,0:T(2,128)(2,1)S(1)}, u32[]{:S(2)}, u32[]{:S(2)}) async-start(bf16[32,2,16384]{2,1,0:T(2,128)(2,1)} %reshape.80), calls=%async_computation | async-start | bytes 4194304 | tf_op jit(solution)/shard_map/all_to_all | solution.py:26
  115.3 383.3 %all-reduce.3.cloned.1.call-start = ((), (), s32[]{:S(2)}) async-start(), calls=%async_computation.2 | async-start | bytes 8388608 | tf_op jit(solution)/shard_map/psum | solution.py:9
  193.2 8.4 %copy-start = (f32[16]{0:T(128)S(1)}, f32[16]{0:T(128)}, u32[]{:S(2)}) copy-start(f32[16]{0:T(128)} %param.5) | copy-start | bytes 196
  193.2 8.4 %copy-start.1 = (s32[16]{0:T(128)S(1)}, s32[16]{0:T(128)}, u32[]{:S(2)}) copy-start(s32[16]{0:T(128)} %param.7) | copy-start | bytes 196
Sparse Core Ops, SparseCore 0:
  10.1 72.0 all-gather.1
  200.2 298.3 all-reduce.2
where the time goes:
time: 653 us; the launch traced here: 652 us
  waiting for transfers between devices  411 us (63%)
  blocking collectives  100 us (15%)
  local copies, waits for them, and re-layouts  84.4 us (13%)
  starting transfers between devices  19.4 us (3%)
  other arithmetic  17.4 us (3%)
  between operations  14.1 us (2%)
    psum x1, waiting for transfers between devices, from_root(): return lax.psum(kept, axis)  284 us
    psum x1, blocking collectives, per_device(): summed = lax.psum(pair_part, ('grp', 'col'))  100 us
    all_gather x1, waiting for transfers between devices, per_device(): gathered = lax.all_gather(reordered, 'grp', axis=0, tiled=True)  74.2 us
    all_to_all x1, waiting for transfers between devices, per_device(): lax.all_to_all(gathered, 'col', split_axis=1, concat_axis=2, tiled=True)  51.6 us
    all_to_all x1, starting transfers between devices, per_device(): lax.all_to_all(gathered, 'col', split_axis=1, concat_axis=2, tiled=True)  19.1 us
    reshape x4, local copies, waits for them, and re-layouts, per_device(): blocks.append(product.reshape(orbitals, width_first, orbitals, width_first))  17.1 us
    unnamed x7, local copies, waits for them, and re-layouts  16.4 us
    reshape x2, local copies, waits for them, and re-layouts, per_device(): partner.reshape(orbitals * width_first, aux_count)  13.5 us
  transfers between devices with their start and end apart: 3, of which 3 were waited for; matrix products, arithmetic and copies ran while one was open for 2% of the time, Pallas kernels for 0%

commit v1 on v0

v1 whole, which is shorter than its diff:
```python
import functools

import jax
import jax.numpy as jnp
import numpy as np
from jax import lax
from jax.experimental import pallas as pl
from jax.experimental.pallas import tpu as pltpu
from jax.sharding import Mesh, PartitionSpec as P

Y, ZL, X, ZH, K = 8, 2, 4, 4, 2
GRP, COL = Y * ZL, X * ZH * K
AUX, NV, NOCC = 2048, 1024, 16
PB = AUX // COL
WA = NV // COL
WB = NV // GRP
ROWS, COLS = NOCC * WA, NOCC * WB
VMEM = pl.BlockSpec(memory_space=pltpu.VMEM)
SMEM = pl.BlockSpec(memory_space=pltpu.SMEM)
PARAMS = pltpu.CompilerParams(vmem_limit_bytes=48 * 1024 * 1024)


def low_half(rows):
    return lax.broadcasted_iota(jnp.int32, (rows, 128), 1) < 64


def turn(v):
    return pltpu.roll(v.astype(jnp.float32), 64, 1).astype(v.dtype)


def pair_halves(first, second):
    low = low_half(first.shape[0])
    return jnp.where(low, first, turn(second)), jnp.where(low, turn(first), second)


def prep_kernel(x_ref, a1_ref, a2_ref):
    low = low_half(WA // 2)
    for t in range(NV // 128):
        tile = x_ref[:, t * 128 : (t + 1) * 128]
        wide = tile.astype(jnp.float32)
        both = jnp.concatenate([wide, wide], axis=0).T
        for s in range(128 // WA):
            top = both[s * WA : s * WA + WA // 2]
            bottom = both[s * WA + WA // 2 : (s + 1) * WA]
            piece = jnp.where(low, top, bottom).astype(jnp.bfloat16)
            c = t * (128 // WA) + s
            for z in range(ZL):
                a1_ref[z * COL + c] = piece
        even, odd = pair_halves(tile[: PB // 2], tile[PB // 2 :])
        for z in range(ZH):
            a2_ref[(2 * t) * ZH + z] = even
            a2_ref[(2 * t + 1) * ZH + z] = odd


def first_kernel(in_ref, out_ref):
    own = lax.axis_index("k")
    for z in range(ZL):
        for rel in range(K):
            k = own if rel == 0 else 1 - own
            for x in range(X):
                for m in range(ZH // 2):
                    base = z * COL + (x * ZH + 2 * m) * K
                    top, bottom = pair_halves(in_ref[base + k], in_ref[base + K + k])
                    lanes = ((rel * X + x) * ZH + 2 * m) * PB
                    out_ref[z, 0 : WA // 2, lanes : lanes + 128] = top
                    out_ref[z, WA // 2 : WA, lanes : lanes + 128] = bottom


def second_kernel(in_ref, out_ref):
    for z in range(ZH):
        for t in range(NOCC // 2):
            top, bottom = pair_halves(in_ref[(2 * t) * ZH + z], in_ref[(2 * t + 1) * ZH + z])
            for copy in range(X):
                out_ref[copy, z, 0 : PB // 2, t * 128 : (t + 1) * 128] = top
                out_ref[copy, z, PB // 2 : PB, t * 128 : (t + 1) * 128] = bottom


def main_kernel(occ_ref, slot_ref, vir_ref, l_ref, r0_ref, r1_ref, perm_ref, amp_ref, energy_ref, x_ref, t_ref, z_ref, col_ref, v_ref):
    column = (lax.axis_index("x") * ZH + lax.axis_index("zh")) * K + lax.axis_index("k")
    group = lax.axis_index("y") * ZL + lax.axis_index("zl")
    half = AUX // 2
    step = 256

    @pl.loop(0, COLS // step)
    def _(n):
        lanes = pl.ds(pl.multiple_of(n * step, step), step)
        x_ref[:, lanes] = jnp.dot(l_ref[:, :half], r0_ref[:, lanes], preferred_element_type=jnp.float32) + jnp.dot(
            l_ref[:, half:], r1_ref[:, lanes], preferred_element_type=jnp.float32
        )

    first_row = vir_ref[pl.ds(column // 4, 1), :]
    v_ref[...] = jnp.broadcast_to(first_row, (128, 128)).T
    col_ref[...] = v_ref[pl.ds(pl.multiple_of((column % 4) * WA, WA), WA), :]
    second_row = vir_ref[pl.ds(group // 2, 1), :]
    low1 = lax.broadcasted_iota(jnp.int32, (1, 128), 1) < 64
    swapped_row = pltpu.roll(jnp.broadcast_to(second_row, (8, 128)), 64, 1)[:1]
    odd = group % 2 == 1
    v_second = jnp.where(low1 != odd, second_row, swapped_row)
    low = low_half(WA)

    @pl.loop(0, NOCC // 2)
    def _(big_j):
        lanes = pl.ds(pl.multiple_of(big_j * 128, 128), 128)
        occ_even = occ_ref[slot_ref[2 * big_j]]
        occ_odd = occ_ref[slot_ref[2 * big_j + 1]]
        second = jnp.where(low1, occ_even, occ_odd) - v_second
        second = second - col_ref[...]
        r0 = pl.multiple_of(big_j * 2 * WA, 2 * WA)
        for big_i in range(NOCC // 2):
            tile = slice(big_i * 128, (big_i + 1) * 128)
            s0 = x_ref[pl.ds(r0, WA), tile]
            s1 = x_ref[pl.ds(r0 + WA, WA), tile]
            swaps = (jnp.where(low, s0, pltpu.roll(s1, 64, 1)), jnp.where(low, pltpu.roll(s0, 64, 1), s1))
            for e in range(2):
                i = 2 * big_i + e
                rows = slice(i * WA, (i + 1) * WA)
                value = x_ref[rows, lanes]
                ratio = value / (second + occ_ref[slot_ref[i]])
                t_ref[rows, lanes] = ratio.astype(jnp.bfloat16)
                part = ratio * (2.0 * value - swaps[e])
                z_ref[i : i + 1, lanes] = jnp.sum(part, axis=0, keepdims=True)

    source = lax.broadcasted_iota(jnp.int32, (COLS, 128), 0) // WB
    target = lax.broadcasted_iota(jnp.int32, (COLS, 128), 1) % NOCC
    chooser = jnp.where(source == target, 1.0, 0.0)
    by_pair = jnp.dot(z_ref[...], chooser, preferred_element_type=jnp.float32, precision=lax.Precision.HIGHEST)
    row = lax.broadcasted_iota(jnp.int32, (NOCC, 128), 0) % 8
    lane = lax.broadcasted_iota(jnp.int32, (NOCC, 128), 1) // NOCC
    kept = jnp.where(row == lane, by_pair, 0.0)
    energy_ref[0:1, :] = jnp.sum(kept[:8], axis=0, keepdims=True)
    energy_ref[1:2, :] = jnp.sum(kept[8:], axis=0, keepdims=True)

    @pl.loop(0, COLS // step)
    def _(n):
        lanes = pl.ds(pl.multiple_of(n * step, step), step)
        amp_ref[:, lanes] = jnp.dot(t_ref[...], perm_ref[:, lanes], preferred_element_type=jnp.float32).astype(jnp.bfloat16)


def permutation():
    source = np.arange(COLS)
    target = (source % WB) * NOCC + source // WB
    matrix = np.zeros((COLS, COLS), np.float32)
    matrix[source, target] = 1.0
    return jnp.asarray(matrix, jnp.bfloat16)


def shape(dims, dtype=jnp.bfloat16):
    return jax.ShapeDtypeStruct(dims, dtype)


def per_device(factors, occ_levels, vir_levels, slot_orbital):
    own = factors.reshape(PB, NV)
    a1, a2 = pl.pallas_call(
        prep_kernel,
        out_shape=(shape((ZL * COL, WA // 2, 128)), shape((GRP * ZH, PB // 2, 128))),
        in_specs=[VMEM],
        out_specs=(VMEM, VMEM),
        compiler_params=PARAMS,
    )(own)
    b1 = lax.all_to_all(a1, ("zl", "x", "zh", "k"), 0, 0, tiled=True)
    first = pl.pallas_call(
        first_kernel,
        out_shape=shape((ZL, WA, AUX)),
        in_specs=[VMEM],
        out_specs=VMEM,
        compiler_params=PARAMS,
    )(b1)
    left = lax.all_gather(first.reshape(ZL * WA, AUX), "y", axis=0, tiled=True)
    a2, _ = lax.optimization_barrier((a2, first))
    b2 = lax.all_to_all(a2, ("y", "zl", "zh"), 0, 0, tiled=True)
    second = pl.pallas_call(
        second_kernel,
        out_shape=shape((X, ZH, PB, COLS)),
        in_specs=[VMEM],
        out_specs=VMEM,
        compiler_params=PARAMS,
    )(b2)
    mine = lax.all_to_all(second.reshape(X, ZH * PB, COLS), "x", 0, 0, tiled=True).reshape(AUX // 2, COLS)
    other = lax.ppermute(mine, "k", [(0, 1), (1, 0)])
    amp, energy = pl.pallas_call(
        main_kernel,
        out_shape=(shape((ROWS, COLS)), shape((2, 128), jnp.float32)),
        in_specs=[SMEM, SMEM, VMEM, VMEM, VMEM, VMEM, VMEM],
        out_specs=(VMEM, VMEM),
        scratch_shapes=[
            pltpu.VMEM((ROWS, COLS), jnp.float32),
            pltpu.VMEM((ROWS, COLS), jnp.bfloat16),
            pltpu.VMEM((NOCC, COLS), jnp.float32),
            pltpu.VMEM((WA, 128), jnp.float32),
            pltpu.VMEM((128, 128), jnp.float32),
        ],
        compiler_params=PARAMS,
    )(occ_levels, slot_orbital, vir_levels.reshape(8, 128), left, mine, other, permutation())
    spread = jnp.broadcast_to(energy[None], (ZL * ZH, 2, 128))
    summed = jnp.sum(lax.all_to_all(spread, ("zl", "zh"), 0, 0, tiled=True), axis=0)
    spread = jnp.broadcast_to(summed[None], (Y * X * K, 2, 128))
    summed = jnp.sum(lax.all_to_all(spread, ("y", "x", "k"), 0, 0, tiled=True), axis=0)
    return amp.reshape(NOCC, WA, COLS), summed.reshape(NOCC, NOCC) / (NV * NV)


def solution(mesh):
    fine = Mesh(mesh.devices.reshape(Y, ZL, X, ZH, K), ("y", "zl", "x", "zh", "k"))
    grp, col = ("y", "zl"), ("x", "zh", "k")
    return jax.shard_map(
        per_device,
        mesh=fine,
        in_specs=(P(col, grp, None), P(), P(), P()),
        out_specs=(P(None, col, grp), P()),
        check_vma=False,
    )
```

time: 653 us -> 164 us (0.25)
  waiting for transfers between devices: 411 us -> 32.5 us
  local copies, waits for them, and re-layouts: 84.4 us -> 3.2 us
  other arithmetic: 17.4 us -> 0.1 us
  Pallas kernels: 0 us -> 12.6 us
  starting transfers between devices: 19.4 us -> 9.94 us
  blocking collectives: 100 us -> 91.3 us
    psum x1 -> x0, waiting for transfers between devices: 284 us -> none  [from_root(): return lax.psum(kept, axis)]
    psum x1 -> x0, blocking collectives: 100 us -> none  [per_device(): summed = lax.psum(pair_part, ('grp', 'col'))]
    all_to_all x0 -> x4, blocking collectives: none -> 91.3 us  [the longest x1 27.4 us: per_device(): b1 = lax.all_to_all(a1, ('zl', 'x', 'zh', 'k'), 0, 0, tiled=True)]
    all_gather x1, waiting for transfers between devices: 74.2 us -> 9.52 us  [per_device(): left = lax.all_gather(first.reshape(ZL * WA, AUX), 'y', axis=0, tiled=True)]
    reshape x7 -> x0, local copies, waits for them, and re-layouts: 36.3 us -> none  [the longest x4 17.1 us: per_device(): blocks.append(product.reshape(orbitals, width_first, orbitals, width_first))]
    all_to_all x1, waiting for transfers between devices: 51.6 us -> 22.2 us  [per_device(): lax.all_to_all(second.reshape(X, ZH * PB, COLS), 'x', 0, 0, tiled=True)]
    all_to_all x1, starting transfers between devices: 19.1 us -> 3.74 us  [per_device(): lax.all_to_all(second.reshape(X, ZH * PB, COLS), 'x', 0, 0, tiled=True)]
    unnamed x7 -> x10, local copies, waits for them, and re-layouts: 16.4 us -> 2.49 us
  transfers between devices with their start and end apart: 3 -> 3, of which waited for: 3 -> 2; matrix products, arithmetic and copies ran while one was open for 2% -> 0% of each run, Pallas kernels for 0% -> 0%
where the time goes in v1:
time: 164 us
  blocking collectives  91.3 us (56%)
  waiting for transfers between devices  32.5 us (20%)
  between operations  14.1 us (9%)
  Pallas kernels  12.6 us (8%)
  starting transfers between devices  9.94 us (6%)
  local copies, waits for them, and re-layouts  3.2 us (2%)
    all_to_all x1, blocking collectives, per_device(): b1 = lax.all_to_all(a1, ('zl', 'x', 'zh', 'k'), 0, 0, tiled=True)  27.4 us
    all_to_all x1, blocking collectives, per_device(): b2 = lax.all_to_all(a2, ('y', 'zl', 'zh'), 0, 0, tiled=True)  27.3 us
    all_to_all x1, blocking collectives, per_device(): lax.all_to_all(spread, ('y', 'x', 'k'), 0, 0, tiled=True)  23.2 us
    all_to_all x1, waiting for transfers between devices, per_device(): lax.all_to_all(second.reshape(X, ZH * PB, COLS), 'x', 0, 0, tiled=True)  22.2 us
    all_to_all x1, blocking collectives, per_device(): lax.all_to_all(spread, ('zl', 'zh'), 0, 0, tiled=True)  13.4 us
    pallas_call x1, Pallas kernels, per_device(): pl.pallas_call(main_kernel, out_shape=(shape((ROWS, COLS)), shape((2, 128...  9.7 us
    all_gather x1, waiting for transfers between devices, per_device(): left = lax.all_gather(first.reshape(ZL * WA, AUX), 'y', axis=0, tiled=True)  9.52 us
    ppermute x1, starting transfers between devices, per_device(): other = lax.ppermute(mine, 'k', [(0, 1), (1, 0)])  6.16 us
  transfers between devices with their start and end apart: 3, of which 2 were waited for; matrix products, arithmetic and copies ran while one was open for 0% of the time, Pallas kernels for 0%

profile of v1, /device:TPU:1, one launch (start us, length us, event | category | flops | bytes accessed | tf_op | source)
XLA Modules:
  0.0 163.7 jit_solution(15380904607931670414)
XLA Ops:
  7.2 0.0 copy-start.1
  7.2 0.9 copy-done.1
  8.1 0.2 shard_map.68
  8.3 27.4 %all_to_all.25.in_ref = bf16[64,16,128]{2,1,0:T(8,128)(2,1)S(1)} all-to-all(bf16[64,16,128]{2,1,0:T(8,128)(2,1)S(1)} %get-tuple-element.7), channel_id=1, replica_groups=mesh['y'=8,'zl'=2,'x'=4,'zh'=4,'k'=2] {'zl','x','zh','k'}, dimensions={0} | all-to-all | bytes 524288 | tf_op jit(solution)/shard_map/all_to_all | solution.py:160
  35.7 0.8 shard_map.69
  36.6 27.3 %all_to_all.26.in_ref = bf16[64,32,128]{2,1,0:T(8,128)(2,1)S(1)} all-to-all(bf16[64,32,128]{2,1,0:T(8,128)(2,1)S(1)} %get-tuple-element.9), channel_id=1, replica_groups=mesh['y'=8,'zl'=2,'x'=4,'zh'=4,'k'=2] {'y','zl','zh'}, dimensions={0} | all-to-all | bytes 1048576 | tf_op jit(solution)/shard_map/all_to_all | solution.py:170
  63.8 1.9 %shard_map.70 = bf16[4,4,64,1024]{3,2,1,0:T(8,128)(2,1)} custom-call(bf16[64,32,128]{2,1,0:T(8,128)(2,1)S(1)} %all_to_all.26.in_ref), custom_call_target="tpu_custom_call" | custom-call | tf_op jit(solution)/shard_map/pallas_call | solution.py:171
  65.7 3.7 %all-to-all-start.2 = ((bf16[4,256,1024]{2,1,0:T(8,128)(2,1)}), bf16[4,256,1024]{2,1,0:T(8,128)(2,1)S(1)}, u32[]{:S(2)}, u32[]{:S(2)}) async-start(bf16[4,256,1024]{2,1,0:T(8,128)(2,1)} %bitcast.3), calls=%async_computation.2 | async-start | bytes 4194304 | tf_op jit(solution)/shard_map/all_to_all | solution.py:178
  69.4 0.0 all-gather.2.cloned.1.call-start
  69.5 0.7 all-gather.2.cloned.1.call-update
  70.2 22.2 %all-to-all-done.2 = bf16[4,256,1024]{2,1,0:T(8,128)(2,1)S(1)} async-done(((bf16[4,256,1024]{2,1,0:T(8,128)(2,1)}), bf16[4,256,1024]{2,1,0:T(8,128)(2,1)S(1)}, u32[]{:S(2)}, u32[]{:S(2)}) %all-to-all-start.2) | async-done | bytes 2097184 | tf_op jit(solution)/shard_map/all_to_all | solution.py:178
  92.4 6.2 %collective-permute-start = (bf16[1024,1024]{1,0:T(8,128)(2,1)S(1)}, bf16[1024,1024]{1,0:T(8,128)(2,1)}, u32[]{:S(2)}, u32[]{:S(2)}) collective-permute-start(bf16[1024,1024]{1,0:T(8,128)(2,1)S(1)} %bitcast.6), channel_id=1, source_target_pairs={{0,1},{1,0},{2,3},{3,2},{4,5},{5,4},{6,7},{7,6},{8,9},{9,8},{10,11... | collective-permute-start | bytes 6291464 | tf_op jit(solution)/shard_map/ppermute | solution.py:179
  98.6 9.5 %all-gather.2.cloned.1.call-done.l_ref = bf16[512,2048]{1,0:T(8,128)(2,1)} async-done(((bf16[64,2048]{1,0:T(8,128)(2,1)}), bf16[512,2048]{1,0:T(8,128)(2,1)}) %all-gather.2.cloned.1.call-update) | async-done | bytes 2097168 | tf_op jit(solution)/shard_map/all_gather | solution.py:168
  108.1 0.0 collective-permute-done.r1_ref
  108.1 0.0 copy-done.2
  108.1 0.0 copy-done.3
  108.1 0.0 copy-done.4
  108.1 0.0 copy-start
  108.1 1.6 copy-done
  109.7 9.7 %shard_map.71 = (bf16[512,1024]{1,0:T(8,128)(2,1)}, f32[2,128]{1,0:T(2,128)S(1)}) custom-call(f32[16]{0:T(128)S(1)} %copy-done.3, s32[16]{0:T(128)S(1)} %copy-done.4, f32[8,128]{1,0:T(8,128)S(1)} %bitcast.9, bf16[512,2048]{1,0:T(8,128)(2,1)S(1)} %copy-done, bf16[1024,1024]{1,0:T(8,128)(2,1)S(1)} %bitcast.7, bf16[1024,1024]{1,0:T(8,128)(2,1)} %collective-permute-done.r1_ref, ...), custom_call_target="tpu_custom_call" | custom-call | tf_op jit(solution)/shard_map/pallas_call | solution.py:180
  119.4 13.4 %all_to_all.27 = f32[8,2,128]{2,1,0:T(2,128)S(1)} all-to-all(f32[8,2,128]{2,1,0:T(2,128)S(1)} %broadcast_in_dim.4), channel_id=1, replica_groups=mesh['y'=8,'zl'=2,'x'=4,'zh'=4,'k'=2] {'zl','zh'}, dimensions={0} | all-to-all | bytes 16384 | tf_op jit(solution)/shard_map/all_to_all | solution.py:195
  132.9 23.2 %all_to_all.28 = f32[64,2,128]{2,1,0:T(2,128)S(1)} all-to-all(f32[64,2,128]{2,1,0:T(2,128)S(1)} %broadcast_in_dim.5), channel_id=1, replica_groups=mesh['y'=8,'zl'=2,'x'=4,'zh'=4,'k'=2] {'y','x','k'}, dimensions={0} | all-to-all | bytes 131072 | tf_op jit(solution)/shard_map/all_to_all | solution.py:197
  156.1 0.1 reduce_sum.19
  156.2 0.7 div.10
  (7 shorter events, 0.1 us)
Async XLA Ops:
  7.2 0.9 copy-start.1
  65.7 42.4 %copy-start.2 = (f32[1024]{0:T(1024)S(1)}, f32[1024]{0:T(1024)}, u32[]{:S(2)}) copy-start(f32[1024]{0:T(1024)} %param.7) | copy-start | bytes 12292
  65.7 42.4 %copy-start.3 = (f32[16]{0:T(128)S(1)}, f32[16]{0:T(128)}, u32[]{:S(2)}) copy-start(f32[16]{0:T(128)} %occ_ref.1) | copy-start | bytes 196
  65.7 42.4 %copy-start.4 = (s32[16]{0:T(128)S(1)}, s32[16]{0:T(128)}, u32[]{:S(2)}) copy-start(s32[16]{0:T(128)} %slot_ref.1) | copy-start | bytes 196
  65.7 26.7 %all-to-all-start.2 = ((bf16[4,256,1024]{2,1,0:T(8,128)(2,1)}), bf16[4,256,1024]{2,1,0:T(8,128)(2,1)S(1)}, u32[]{:S(2)}, u32[]{:S(2)}) async-start(bf16[4,256,1024]{2,1,0:T(8,128)(2,1)} %bitcast.3), calls=%async_computation.2 | async-start | bytes 4194304 | tf_op jit(solution)/shard_map/all_to_all | solution.py:178
  69.4 38.7 %all-gather.2.cloned.1.call-start = ((), (), s32[]{:S(2)}) async-start(), calls=%async_computation.5 | async-start | bytes 2359296 | tf_op jit(solution)/shard_map/all_gather | solution.py:168
  92.4 15.7 %collective-permute-start = (bf16[1024,1024]{1,0:T(8,128)(2,1)S(1)}, bf16[1024,1024]{1,0:T(8,128)(2,1)}, u32[]{:S(2)}, u32[]{:S(2)}) collective-permute-start(bf16[1024,1024]{1,0:T(8,128)(2,1)S(1)} %bitcast.6), channel_id=1, source_target_pairs={{0,1},{1,0},{2,3},{3,2},{4,5},{5,4},{6,7},{7,6},{8,9},{9,8},{10,11... | collective-permute-start | bytes 6291464 | tf_op jit(solution)/shard_map/ppermute | solution.py:179
  108.1 1.6 copy-start
Sparse Core Ops, SparseCore 0:
  72.9 35.1 all-gather.1

commit v2 on v1

--- a/solution.py
+++ b/solution.py
@@ -75,19 +75,9 @@
                 out_ref[copy, z, PB // 2 : PB, t * 128 : (t + 1) * 128] = bottom
 
 
-def main_kernel(occ_ref, slot_ref, vir_ref, l_ref, r0_ref, r1_ref, perm_ref, amp_ref, energy_ref, x_ref, t_ref, z_ref, col_ref, v_ref):
+def inverse_kernel(occ_ref, slot_ref, vir_ref, inv_ref, col_ref, v_ref):
     column = (lax.axis_index("x") * ZH + lax.axis_index("zh")) * K + lax.axis_index("k")
     group = lax.axis_index("y") * ZL + lax.axis_index("zl")
-    half = AUX // 2
-    step = 256
-
-    @pl.loop(0, COLS // step)
-    def _(n):
-        lanes = pl.ds(pl.multiple_of(n * step, step), step)
-        x_ref[:, lanes] = jnp.dot(l_ref[:, :half], r0_ref[:, lanes], preferred_element_type=jnp.float32) + jnp.dot(
-            l_ref[:, half:], r1_ref[:, lanes], preferred_element_type=jnp.float32
-        )
-
     first_row = vir_ref[pl.ds(column // 4, 1), :]
     v_ref[...] = jnp.broadcast_to(first_row, (128, 128)).T
     col_ref[...] = v_ref[pl.ds(pl.multiple_of((column % 4) * WA, WA), WA), :]
@@ -96,15 +86,33 @@
     swapped_row = pltpu.roll(jnp.broadcast_to(second_row, (8, 128)), 64, 1)[:1]
     odd = group % 2 == 1
     v_second = jnp.where(low1 != odd, second_row, swapped_row)
-    low = low_half(WA)
 
     @pl.loop(0, NOCC // 2)
     def _(big_j):
         lanes = pl.ds(pl.multiple_of(big_j * 128, 128), 128)
         occ_even = occ_ref[slot_ref[2 * big_j]]
         occ_odd = occ_ref[slot_ref[2 * big_j + 1]]
-        second = jnp.where(low1, occ_even, occ_odd) - v_second
-        second = second - col_ref[...]
+        second = jnp.where(low1, occ_even, occ_odd) - v_second - col_ref[...]
+        for i in range(NOCC):
+            inv_ref[i * WA : (i + 1) * WA, lanes] = 1.0 / (second + occ_ref[slot_ref[i]])
+
+
+def main_kernel(l_ref, r0_ref, r1_ref, inv_ref, amp_ref, energy_ref, x_ref, z_ref):
+    half = AUX // 2
+    step = 256
+
+    @pl.loop(0, COLS // step)
+    def _(n):
+        lanes = pl.ds(pl.multiple_of(n * step, step), step)
+        x_ref[:, lanes] = jnp.dot(l_ref[:, :half], r0_ref[:, lanes], preferred_element_type=jnp.float32) + jnp.dot(
+            l_ref[:, half:], r1_ref[:, lanes], preferred_element_type=jnp.float32
+        )
+
+    low = low_half(WA)
+
+    @pl.loop(0, NOCC // 2)
+    def _(big_j):
+        lanes = pl.ds(pl.multiple_of(big_j * 128, 128), 128)
         r0 = pl.multiple_of(big_j * 2 * WA, 2 * WA)
         for big_i in range(NOCC // 2):
             tile = slice(big_i * 128, (big_i + 1) * 128)
@@ -115,8 +123,8 @@
                 i = 2 * big_i + e
                 rows = slice(i * WA, (i + 1) * WA)
                 value = x_ref[rows, lanes]
-                ratio = value / (second + occ_ref[slot_ref[i]])
-                t_ref[rows, lanes] = ratio.astype(jnp.bfloat16)
+                ratio = value * inv_ref[rows, lanes]
+                amp_ref[rows, lanes] = ratio.astype(jnp.bfloat16)
                 part = ratio * (2.0 * value - swaps[e])
                 z_ref[i : i + 1, lanes] = jnp.sum(part, axis=0, keepdims=True)
 
@@ -130,6 +138,10 @@
     energy_ref[0:1, :] = jnp.sum(kept[:8], axis=0, keepdims=True)
     energy_ref[1:2, :] = jnp.sum(kept[8:], axis=0, keepdims=True)
 
+
+def order_kernel(t_ref, perm_ref, amp_ref):
+    step = 256
+
     @pl.loop(0, COLS // step)
     def _(n):
         lanes = pl.ds(pl.multiple_of(n * step, step), step)
@@ -176,21 +188,33 @@
         compiler_params=PARAMS,
     )(b2)
     mine = lax.all_to_all(second.reshape(X, ZH * PB, COLS), "x", 0, 0, tiled=True).reshape(AUX // 2, COLS)
+    mine, left = lax.optimization_barrier((mine, left))
     other = lax.ppermute(mine, "k", [(0, 1), (1, 0)])
-    amp, energy = pl.pallas_call(
+    inverse = pl.pallas_call(
+        inverse_kernel,
+        out_shape=shape((ROWS, COLS), jnp.float32),
+        in_specs=[SMEM, SMEM, VMEM],
+        out_specs=VMEM,
+        scratch_shapes=[pltpu.VMEM((WA, 128), jnp.float32), pltpu.VMEM((128, 128), jnp.float32)],
+        compiler_params=PARAMS,
+        cost_estimate=pl.CostEstimate(flops=ROWS * COLS * 10, bytes_accessed=4 * ROWS * COLS * 4, transcendentals=0),
+    )(occ_levels, slot_orbital, vir_levels.reshape(8, 128))
+    ratio, energy = pl.pallas_call(
         main_kernel,
         out_shape=(shape((ROWS, COLS)), shape((2, 128), jnp.float32)),
-        in_specs=[SMEM, SMEM, VMEM, VMEM, VMEM, VMEM, VMEM],
+        in_specs=[VMEM, VMEM, VMEM, VMEM],
         out_specs=(VMEM, VMEM),
-        scratch_shapes=[
-            pltpu.VMEM((ROWS, COLS), jnp.float32),
-            pltpu.VMEM((ROWS, COLS), jnp.bfloat16),
-            pltpu.VMEM((NOCC, COLS), jnp.float32),
-            pltpu.VMEM((WA, 128), jnp.float32),
-            pltpu.VMEM((128, 128), jnp.float32),
-        ],
-        compiler_params=PARAMS,
-    )(occ_levels, slot_orbital, vir_levels.reshape(8, 128), left, mine, other, permutation())
+        scratch_shapes=[pltpu.VMEM((ROWS, COLS), jnp.float32), pltpu.VMEM((NOCC, COLS), jnp.float32)],
+        compiler_params=PARAMS,
+    )(left, mine, other, inverse)
+    amp = pl.pallas_call(
+        order_kernel,
+        out_shape=shape((ROWS, COLS)),
+        in_specs=[VMEM, VMEM],
+        out_specs=VMEM,
+        compiler_params=PARAMS,
+        cost_estimate=pl.CostEstimate(flops=2 * ROWS * COLS * COLS, bytes_accessed=2 * COLS * COLS + 4 * ROWS * COLS, transcendentals=0),
+    )(ratio, permutation())
     spread = jnp.broadcast_to(energy[None], (ZL * ZH, 2, 128))
     summed = jnp.sum(lax.all_to_all(spread, ("zl", "zh"), 0, 0, tiled=True), axis=0)
     spread = jnp.broadcast_to(summed[None], (Y * X * K, 2, 128))

time: 164 us -> 148 us (0.902)
  waiting for transfers between devices: 32.5 us -> 7.06 us
  starting transfers between devices: 9.94 us -> 14.2 us
  local copies, waits for them, and re-layouts: 3.2 us -> 6.48 us
  blocking collectives: 91.3 us -> 93.2 us
    all_to_all x1, waiting for transfers between devices: 22.2 us -> 5.72 us  [per_device(): lax.all_to_all(spread, ('y', 'x', 'k'), 0, 0, tiled=True)]
    all_gather x1, waiting for transfers between devices: 9.52 us -> 0.01 us  [per_device(): left = lax.all_gather(first.reshape(ZL * WA, AUX), 'y', axis=0, tiled=True)]
    pallas_call x0 -> x2, Pallas kernels: none -> 3.85 us  [the longest x1 2.77 us: per_device(): pl.pallas_call(order_kernel, out_shape=shape((ROWS, COLS)), in_specs=[VME...]
    all_to_all x1, blocking collectives: 27.3 us -> 31 us  [per_device(): b2 = lax.all_to_all(a2, ('y', 'zl', 'zh'), 0, 0, tiled=True)]
    pallas_call x1, Pallas kernels: 9.7 us -> 6.83 us  [per_device(): pl.pallas_call(main_kernel, out_shape=(shape((ROWS, COLS)), shape((2, 128...]
    unnamed x10 -> x16, local copies, waits for them, and re-layouts: 2.49 us -> 5.15 us
    all_to_all x1, blocking collectives: 13.4 us -> 11 us  [per_device(): lax.all_to_all(spread, ('zl', 'zh'), 0, 0, tiled=True)]
    all_to_all x1, starting transfers between devices: 3.74 us -> 6.09 us  [per_device(): lax.all_to_all(spread, ('y', 'x', 'k'), 0, 0, tiled=True)]
  transfers between devices with their start and end apart: 3 -> 3, of which waited for: 2 -> 2; matrix products, arithmetic and copies ran while one was open for 0% -> 0% of each run, Pallas kernels for 0% -> 3%
where the time goes in v2:
time: 148 us; the launch traced here: 147 us
  blocking collectives  93.2 us (63%)
  starting transfers between devices  14.2 us (10%)
  between operations  14.2 us (10%)
  Pallas kernels  12.3 us (8%)
  waiting for transfers between devices  7.06 us (5%)
  local copies, waits for them, and re-layouts  6.48 us (4%)
    all_to_all x1, blocking collectives, per_device(): b2 = lax.all_to_all(a2, ('y', 'zl', 'zh'), 0, 0, tiled=True)  31 us
    all_to_all x1, blocking collectives, per_device(): b1 = lax.all_to_all(a1, ('zl', 'x', 'zh', 'k'), 0, 0, tiled=True)  27.4 us
    all_to_all x1, blocking collectives, per_device(): lax.all_to_all(second.reshape(X, ZH * PB, COLS), 'x', 0, 0, tiled=True)  23.8 us
    all_to_all x1, blocking collectives, per_device(): lax.all_to_all(spread, ('zl', 'zh'), 0, 0, tiled=True)  11 us
    ppermute x1, starting transfers between devices, per_device(): other = lax.ppermute(mine, 'k', [(0, 1), (1, 0)])  8.09 us
    pallas_call x1, Pallas kernels, per_device(): pl.pallas_call(main_kernel, out_shape=(shape((ROWS, COLS)), shape((2, 128...  6.83 us
    all_to_all x1, starting transfers between devices, per_device(): lax.all_to_all(spread, ('y', 'x', 'k'), 0, 0, tiled=True)  6.09 us
    all_to_all x1, waiting for transfers between devices, per_device(): lax.all_to_all(spread, ('y', 'x', 'k'), 0, 0, tiled=True)  5.72 us
  transfers between devices with their start and end apart: 3, of which 2 were waited for; matrix products, arithmetic and copies ran while one was open for 0% of the time, Pallas kernels for 3%

profile of v2, /device:TPU:1, one launch (start us, length us, event | category | flops | bytes accessed | tf_op | source)
XLA Modules:
  0.0 147.5 jit_solution(990721662890580247)
XLA Ops:
  7.2 0.0 all-gather.2.cloned.1.call-start
  7.2 0.9 copy-done.3
  8.1 0.2 shard_map.68
  8.3 27.4 %all_to_all.25.in_ref = bf16[64,16,128]{2,1,0:T(8,128)(2,1)S(1)} all-to-all(bf16[64,16,128]{2,1,0:T(8,128)(2,1)S(1)} %get-tuple-element.10), channel_id=1, replica_groups=mesh['y'=8,'zl'=2,'x'=4,'zh'=4,'k'=2] {'zl','x','zh','k'}, dimensions={0} | all-to-all | bytes 524288 | tf_op jit(solution)/shard_map/all_to_all | solution.py:172
  35.8 0.8 shard_map.69
  36.6 0.0 all-gather.2.cloned.1.call-update
  36.6 31.0 %all_to_all.26.in_ref = bf16[64,32,128]{2,1,0:T(8,128)(2,1)S(1)} all-to-all(bf16[64,32,128]{2,1,0:T(8,128)(2,1)S(1)} %get-tuple-element.11), channel_id=1, replica_groups=mesh['y'=8,'zl'=2,'x'=4,'zh'=4,'k'=2] {'y','zl','zh'}, dimensions={0} | all-to-all | bytes 1048576 | tf_op jit(solution)/shard_map/all_to_all | solution.py:182
  67.6 0.5 shard_map.70
  68.2 23.8 %all_to_all.27 = bf16[4,256,1024]{2,1,0:T(8,128)(2,1)S(1)} all-to-all(bf16[4,256,1024]{2,1,0:T(8,128)(2,1)S(1)} %bitcast.6), channel_id=1, replica_groups=mesh['y'=8,'zl'=2,'x'=4,'zh'=4,'k'=2] {'x'}, dimensions={0} | all-to-all | bytes 4194304 | tf_op jit(solution)/shard_map/all_to_all | solution.py:190
  92.0 8.1 %collective-permute-start = (bf16[1024,1024]{1,0:T(8,128)(2,1)S(1)}, bf16[1024,1024]{1,0:T(8,128)(2,1)S(1)}, u32[]{:S(2)}, u32[]{:S(2)}) collective-permute-start(bf16[1024,1024]{1,0:T(8,128)(2,1)S(1)} %bitcast.7), channel_id=1, source_target_pairs={{0,1},{1,0},{2,3},{3,2},{4,5},{5,4},{6,7},{7,6},{8,9},{9,8},{10,11... | collective-permute-start | bytes 6291464 | tf_op jit(solution)/shard_map/ppermute | solution.py:192
  100.1 1.1 shard_map.71.inv_ref
  101.2 1.3 copy-done
  102.5 1.3 collective-permute-done.r1_ref
  103.9 1.3 copy-done.7
  105.2 6.8 %shard_map.72 = (bf16[512,1024]{1,0:T(8,128)(2,1)S(1)}, f32[2,128]{1,0:T(2,128)S(1)}) custom-call(bf16[512,2048]{1,0:T(8,128)(2,1)S(1)} %copy-done.2, bf16[1024,1024]{1,0:T(8,128)(2,1)S(1)} %bitcast.8, bf16[1024,1024]{1,0:T(8,128)(2,1)} %copy-done.7, f32[512,1024]{1,0:T(8,128)} %copy-done), custom_call_target="tpu_custom_call" | custom-call | tf_op jit(solution)/shard_map/pallas_call | solution.py:202
  112.0 11.0 %all_to_all.28 = f32[8,2,128]{2,1,0:T(2,128)S(1)} all-to-all(f32[8,2,128]{2,1,0:T(2,128)S(1)} %broadcast_in_dim.4), channel_id=1, replica_groups=mesh['y'=8,'zl'=2,'x'=4,'zh'=4,'k'=2] {'zl','zh'}, dimensions={0} | all-to-all | bytes 16384 | tf_op jit(solution)/shard_map/all_to_all | solution.py:219
  123.0 0.6 broadcast_in_dim.5
  123.7 6.1 %all-to-all-start.4 = ((f32[64,2,128]{2,1,0:T(2,128)}), f32[64,2,128]{2,1,0:T(2,128)S(1)}, u32[]{:S(2)}, u32[]{:S(2)}) async-start(f32[64,2,128]{2,1,0:T(2,128)} %broadcast_in_dim.5), calls=%async_computation.4 | async-start | bytes 131072 | tf_op jit(solution)/shard_map/all_to_all | solution.py:221
  129.8 0.0 copy-start.1
  129.8 1.6 %copy-done.1 = bf16[1024,1024]{1,0:T(8,128)(2,1)S(1)} copy-done((bf16[1024,1024]{1,0:T(8,128)(2,1)S(1)}, bf16[1024,1024]{1,0:T(8,128)(2,1)}, u32[]{:S(2)}) %copy-start.1) | copy-done | bytes 2097176
  131.4 2.8 %shard_map.73 = bf16[512,1024]{1,0:T(8,128)(2,1)} custom-call(bf16[512,1024]{1,0:T(8,128)(2,1)S(1)} %get-tuple-element.14.t_ref, bf16[1024,1024]{1,0:T(8,128)(2,1)S(1)} %copy-done.1), custom_call_target="tpu_custom_call" | custom-call | flops 1073741824 | bytes 4194304 | tf_op jit(solution)/shard_map/pallas_call | solution.py:210
  134.2 5.7 %all-to-all-done.4 = f32[64,2,128]{2,1,0:T(2,128)S(1)} async-done(((f32[64,2,128]{2,1,0:T(2,128)}), f32[64,2,128]{2,1,0:T(2,128)S(1)}, u32[]{:S(2)}, u32[]{:S(2)}) %all-to-all-start.4) | async-done | bytes 65568 | tf_op jit(solution)/shard_map/all_to_all | solution.py:221
  139.9 0.1 reduce_sum.19
  140.0 0.7 div.10
  (15 shorter events, 0.1 us)
Async XLA Ops:
  7.2 84.8 %all-gather.2.cloned.1.call-start = ((), (), s32[]{:S(2)}) async-start(), calls=%async_computation.5 | async-start | bytes 2359296 | tf_op jit(solution)/shard_map/all_gather | solution.py:180
  7.2 0.9 copy-start.3
  68.1 32.0 %copy-start.4 = (f32[1024]{0:T(1024)S(1)}, f32[1024]{0:T(1024)}, u32[]{:S(2)}) copy-start(f32[1024]{0:T(1024)} %param.7) | copy-start | bytes 12292
  68.1 32.0 %copy-start.5 = (f32[16]{0:T(128)S(1)}, f32[16]{0:T(128)}, u32[]{:S(2)}) copy-start(f32[16]{0:T(128)} %occ_ref.1) | copy-start | bytes 196
  68.2 32.0 %copy-start.6 = (s32[16]{0:T(128)S(1)}, s32[16]{0:T(128)}, u32[]{:S(2)}) copy-start(s32[16]{0:T(128)} %slot_ref.1) | copy-start | bytes 196
  92.0 13.2 %copy-start.2 = (bf16[512,2048]{1,0:T(8,128)(2,1)S(1)}, bf16[512,2048]{1,0:T(8,128)(2,1)}, u32[]{:S(2)}) copy-start(bf16[512,2048]{1,0:T(8,128)(2,1)} %all-gather.2.cloned.1.call-done.l_ref) | copy-start | bytes 6291460
  92.0 11.9 %collective-permute-start = (bf16[1024,1024]{1,0:T(8,128)(2,1)S(1)}, bf16[1024,1024]{1,0:T(8,128)(2,1)S(1)}, u32[]{:S(2)}, u32[]{:S(2)}) collective-permute-start(bf16[1024,1024]{1,0:T(8,128)(2,1)S(1)} %bitcast.7), channel_id=1, source_target_pairs={{0,1},{1,0},{2,3},{3,2},{4,5},{5,4},{6,7},{7,6},{8,9},{9,8},{10,11... | collective-permute-start | bytes 6291464 | tf_op jit(solution)/shard_map/ppermute | solution.py:192
  101.2 1.3 copy-start
  103.9 1.3 copy-start.7
  123.7 16.2 %all-to-all-start.4 = ((f32[64,2,128]{2,1,0:T(2,128)}), f32[64,2,128]{2,1,0:T(2,128)S(1)}, u32[]{:S(2)}, u32[]{:S(2)}) async-start(f32[64,2,128]{2,1,0:T(2,128)} %broadcast_in_dim.5), calls=%async_computation.4 | async-start | bytes 131072 | tf_op jit(solution)/shard_map/all_to_all | solution.py:221
  129.8 1.6 %copy-start.1 = (bf16[1024,1024]{1,0:T(8,128)(2,1)S(1)}, bf16[1024,1024]{1,0:T(8,128)(2,1)}, u32[]{:S(2)}) copy-start(bf16[1024,1024]{1,0:T(8,128)(2,1)} %constant.7.clone.perm_ref) | copy-start | bytes 6291460
Sparse Core Ops, SparseCore 0:
  36.7 45.7 all-gather.1

commit v3 on v2

v3 whole, which is shorter than its diff:
```python
import jax
import jax.numpy as jnp
import numpy as np
from jax import lax
from jax.experimental import pallas as pl
from jax.experimental.pallas import tpu as pltpu
from jax.sharding import Mesh, PartitionSpec as P

Y, ZL, X, ZH, K = 8, 2, 4, 4, 2
GRP, COL = Y * ZL, X * ZH * K
AUX, NV, NOCC = 2048, 1024, 16
PB = AUX // COL
WA = NV // COL
WB = NV // GRP
ROWS, COLS = NOCC * WA, NOCC * WB
STEP = 256
VMEM = pl.BlockSpec(memory_space=pltpu.VMEM)
SMEM = pl.BlockSpec(memory_space=pltpu.SMEM)
PARAMS = pltpu.CompilerParams(vmem_limit_bytes=16 * 1024 * 1024)


def low_half(rows):
    return lax.broadcasted_iota(jnp.int32, (rows, 128), 1) < 64


def turn(v):
    return pltpu.roll(v.astype(jnp.float32), 64, 1).astype(v.dtype)


def pair_halves(first, second):
    low = low_half(first.shape[0])
    return jnp.where(low, first, turn(second)), jnp.where(low, turn(first), second)


def prep_kernel(x_ref, a1_ref, a2_ref):
    low = low_half(WA // 2)
    for t in range(NV // 128):
        tile = x_ref[:, t * 128 : (t + 1) * 128]
        wide = tile.astype(jnp.float32)
        both = jnp.concatenate([wide, wide], axis=0).T
        for s in range(128 // WA):
            top = both[s * WA : s * WA + WA // 2]
            bottom = both[s * WA + WA // 2 : (s + 1) * WA]
            piece = jnp.where(low, top, bottom).astype(jnp.bfloat16)
            c = t * (128 // WA) + s
            for z in range(ZL):
                a1_ref[z * COL + c] = piece
        even, odd = pair_halves(tile[: PB // 2], tile[PB // 2 :])
        a2_ref[2 * t] = even
        a2_ref[2 * t + 1] = odd


def first_kernel(in_ref, out_ref):
    own = lax.axis_index("k")
    for z in range(ZL):
        for rel in range(K):
            k = own if rel == 0 else 1 - own
            for x in range(X):
                for m in range(ZH // 2):
                    base = z * COL + (x * ZH + 2 * m) * K
                    top, bottom = pair_halves(in_ref[base + k], in_ref[base + K + k])
                    lanes = ((rel * X + x) * ZH + 2 * m) * PB
                    out_ref[z, 0 : WA // 2, lanes : lanes + 128] = top
                    out_ref[z, WA // 2 : WA, lanes : lanes + 128] = bottom


def second_kernel(in_ref, out_ref):
    for t in range(NOCC // 2):
        top, bottom = pair_halves(in_ref[2 * t], in_ref[2 * t + 1])
        out_ref[0 : PB // 2, t * 128 : (t + 1) * 128] = top
        out_ref[PB // 2 : PB, t * 128 : (t + 1) * 128] = bottom


def inverse_kernel(occ_ref, slot_ref, vir_ref, inv_ref, col_ref, v_ref):
    column = (lax.axis_index("x") * ZH + lax.axis_index("zh")) * K + lax.axis_index("k")
    group = lax.axis_index("y") * ZL + lax.axis_index("zl")
    first_row = vir_ref[pl.ds(column // 4, 1), :]
    v_ref[...] = jnp.broadcast_to(first_row, (128, 128)).T
    col_ref[...] = v_ref[pl.ds(pl.multiple_of((column % 4) * WA, WA), WA), :]
    second_row = vir_ref[pl.ds(group // 2, 1), :]
    low1 = lax.broadcasted_iota(jnp.int32, (1, 128), 1) < 64
    swapped_row = pltpu.roll(jnp.broadcast_to(second_row, (8, 128)), 64, 1)[:1]
    odd = group % 2 == 1
    v_second = jnp.where(low1 != odd, second_row, swapped_row)

    @pl.loop(0, NOCC // 2)
    def _(big_j):
        lanes = pl.ds(pl.multiple_of(big_j * 128, 128), 128)
        occ_even = occ_ref[slot_ref[2 * big_j]]
        occ_odd = occ_ref[slot_ref[2 * big_j + 1]]
        second = jnp.where(low1, occ_even, occ_odd) - v_second - col_ref[...]
        for i in range(NOCC):
            inv_ref[i * WA : (i + 1) * WA, lanes] = 1.0 / (second + occ_ref[slot_ref[i]])


def half_kernel(l_ref, r_ref, x_ref):
    @pl.loop(0, COLS // STEP)
    def _(n):
        lanes = pl.ds(pl.multiple_of(n * STEP, STEP), STEP)
        x_ref[:, lanes] = jnp.dot(l_ref[:, : AUX // 2], r_ref[:, lanes], preferred_element_type=jnp.float32)


def main_kernel(half_ref, l_ref, r_ref, inv_ref, amp_ref, energy_ref, x_ref, z_ref):
    @pl.loop(0, COLS // STEP)
    def _(n):
        lanes = pl.ds(pl.multiple_of(n * STEP, STEP), STEP)
        x_ref[:, lanes] = half_ref[:, lanes] + jnp.dot(l_ref[:, AUX // 2 :], r_ref[:, lanes], preferred_element_type=jnp.float32)

    low = low_half(WA)

    @pl.loop(0, NOCC // 2)
    def _(big_j):
        lanes = pl.ds(pl.multiple_of(big_j * 128, 128), 128)
        r0 = pl.multiple_of(big_j * 2 * WA, 2 * WA)
        for big_i in range(NOCC // 2):
            tile = slice(big_i * 128, (big_i + 1) * 128)
            s0 = x_ref[pl.ds(r0, WA), tile]
            s1 = x_ref[pl.ds(r0 + WA, WA), tile]
            swaps = (jnp.where(low, s0, pltpu.roll(s1, 64, 1)), jnp.where(low, pltpu.roll(s0, 64, 1), s1))
            for e in range(2):
                i = 2 * big_i + e
                rows = slice(i * WA, (i + 1) * WA)
                value = x_ref[rows, lanes]
                ratio = value * inv_ref[rows, lanes]
                amp_ref[rows, lanes] = ratio.astype(jnp.bfloat16)
                part = ratio * (2.0 * value - swaps[e])
                z_ref[i * 8 : (i + 1) * 8, lanes] = jnp.sum(part.reshape(WA // 8, 8, 128), axis=0)

    source = lax.broadcasted_iota(jnp.int32, (COLS, 128), 0) // WB
    target = lax.broadcasted_iota(jnp.int32, (COLS, 128), 1) % NOCC
    chooser = jnp.where(source == target, 1.0, 0.0)
    by_pair = jnp.dot(z_ref[...], chooser, preferred_element_type=jnp.float32, precision=lax.Precision.HIGHEST)
    row = (lax.broadcasted_iota(jnp.int32, (NOCC * 8, 128), 0) // 8) % 8
    lane = lax.broadcasted_iota(jnp.int32, (NOCC * 8, 128), 1) // NOCC
    kept = jnp.where(row == lane, by_pair, 0.0)
    halves = [jnp.sum(kept[h * 64 : (h + 1) * 64], axis=0, keepdims=True) for h in range(2)]
    energy = jnp.concatenate(halves, axis=0)
    for z in range(ZL * ZH):
        energy_ref[z] = energy


def middle_kernel(in_ref, out_ref):
    total = jnp.sum(in_ref[...], axis=0)
    for n in range(Y * X * K):
        out_ref[n] = total


def last_kernel(in_ref, out_ref):
    total = jnp.sum(in_ref[...], axis=0) * (1.0 / (NV * NV))
    rows = jnp.concatenate([jnp.broadcast_to(total[h : h + 1], (8, 128)) for h in range(2)], axis=0)
    row = lax.broadcasted_iota(jnp.int32, (NOCC, 128), 0) % 8
    lane = lax.broadcasted_iota(jnp.int32, (NOCC, 128), 1) // NOCC
    kept = jnp.where(row == lane, rows, 0.0)
    source = lax.broadcasted_iota(jnp.int32, (128, NOCC), 0) % NOCC
    target = lax.broadcasted_iota(jnp.int32, (128, NOCC), 1)
    chooser = jnp.where(source == target, 1.0, 0.0)
    out_ref[...] = jnp.dot(kept, chooser, preferred_element_type=jnp.float32, precision=lax.Precision.HIGHEST)


def order_kernel(t_ref, perm_ref, amp_ref):
    @pl.loop(0, COLS // STEP)
    def _(n):
        lanes = pl.ds(pl.multiple_of(n * STEP, STEP), STEP)
        amp_ref[:, lanes] = jnp.dot(t_ref[...], perm_ref[:, lanes], preferred_element_type=jnp.float32).astype(jnp.bfloat16)


def permutation():
    source = np.arange(COLS)
    target = (source % WB) * NOCC + source // WB
    matrix = np.zeros((COLS, COLS), np.float32)
    matrix[source, target] = 1.0
    return jnp.asarray(matrix, jnp.bfloat16)


def shape(dims, dtype=jnp.bfloat16):
    return jax.ShapeDtypeStruct(dims, dtype)


def call(kernel, out_shape, operands, in_specs=None, scratch=(), flops=0):
    kinds = in_specs or [VMEM] * len(operands)
    cost = pl.CostEstimate(flops=flops, bytes_accessed=4 * ROWS * COLS, transcendentals=0) if flops else None
    return pl.pallas_call(
        kernel,
        out_shape=out_shape,
        in_specs=kinds,
        out_specs=jax.tree.map(lambda _: VMEM, out_shape),
        scratch_shapes=scratch,
        compiler_params=PARAMS,
        cost_estimate=cost,
    )(*operands)


def per_device(factors, occ_levels, vir_levels, slot_orbital):
    f32 = jnp.float32
    a1, a2 = call(
        prep_kernel,
        (shape((ZL * COL, WA // 2, 128)), shape((GRP, PB // 2, 128))),
        [factors.reshape(PB, NV)],
    )
    b1 = lax.all_to_all(a1, ("zl", "x", "zh", "k"), 0, 0, tiled=True)
    first = call(first_kernel, shape((ZL, WA, AUX)), [b1])
    left = lax.all_gather(first.reshape(ZL * WA, AUX), "y", axis=0, tiled=True)
    a2, _ = lax.optimization_barrier((a2, first))
    b2 = lax.all_to_all(a2, ("y", "zl"), 0, 0, tiled=True)
    second = call(second_kernel, shape((PB, COLS)), [b2])
    second = lax.all_gather(second, "zh", axis=0, tiled=True)
    spread = jnp.broadcast_to(second[None], (X, ZH * PB, COLS))
    mine = lax.all_to_all(spread, "x", 0, 0, tiled=True).reshape(AUX // 2, COLS)
    mine, left = lax.optimization_barrier((mine, left))
    other = lax.ppermute(mine, "k", [(0, 1), (1, 0)])
    inverse = call(
        inverse_kernel,
        shape((ROWS, COLS), f32),
        [occ_levels, slot_orbital, vir_levels.reshape(8, 128)],
        in_specs=[SMEM, SMEM, VMEM],
        scratch=[pltpu.VMEM((WA, 128), f32), pltpu.VMEM((128, 128), f32)],
        flops=ROWS * COLS * 10,
    )
    half = call(half_kernel, shape((ROWS, COLS), f32), [left, mine], flops=ROWS * COLS * AUX)
    ratio, energy = call(
        main_kernel,
        (shape((ROWS, COLS)), shape((ZL * ZH, 2, 128), f32)),
        [half, left, other, inverse],
        scratch=[pltpu.VMEM((ROWS, COLS), f32), pltpu.VMEM((NOCC * 8, COLS), f32)],
    )
    amp = call(order_kernel, shape((ROWS, COLS)), [ratio, permutation()], flops=2 * ROWS * COLS * COLS)
    energy = lax.all_to_all(energy, ("zl", "zh"), 0, 0, tiled=True)
    energy = call(middle_kernel, shape((Y * X * K, 2, 128), f32), [energy])
    energy = lax.all_to_all(energy, ("y", "x", "k"), 0, 0, tiled=True)
    return amp.reshape(NOCC, WA, COLS), call(last_kernel, shape((NOCC, NOCC), f32), [energy])


def solution(mesh):
    fine = Mesh(mesh.devices.reshape(Y, ZL, X, ZH, K), ("y", "zl", "x", "zh", "k"))
    grp, col = ("y", "zl"), ("x", "zh", "k")
    return jax.shard_map(
        per_device,
        mesh=fine,
        in_specs=(P(col, grp, None), P(), P(), P()),
        out_specs=(P(None, col, grp), P()),
        check_vma=False,
    )
```

time: 148 us -> 142 us (0.959)
  local copies, waits for them, and re-layouts: 6.48 us -> 1.18 us
    all_to_all x3, blocking collectives: 65.8 us -> 50.3 us  [the longest x1 24.3 us: per_device(): mine = lax.all_to_all(spread, 'x', 0, 0, tiled=True).reshape(AUX // 2, COLS)]
    all_gather x0 -> x1, blocking collectives: none -> 14.4 us  [per_device(): second = lax.all_gather(second, 'zh', axis=0, tiled=True)]
    unnamed x16 -> x12, local copies, waits for them, and re-layouts: 5.15 us -> 0.92 us
    all_to_all x1, waiting for transfers between devices: 5.72 us -> 7.31 us  [per_device(): energy = lax.all_to_all(energy, ('y', 'x', 'k'), 0, 0, tiled=True)]
    pallas_call x6 -> x9, Pallas kernels: 12.3 us -> 11.9 us  [call(): pl.pallas_call(kernel, out_shape=out_shape, in_specs=kinds, out_specs=jax...]
  transfers between devices with their start and end apart: 3 -> 3, of which waited for: 2 -> 2; matrix products, arithmetic and copies ran while one was open for 0% -> 0% of each run, Pallas kernels for 3% -> 4%
where the time goes in v3:
time: 142 us; the launch traced here: 141 us
  blocking collectives  92.1 us (65%)
  between operations  14.2 us (10%)
  starting transfers between devices  13.6 us (10%)
  Pallas kernels  11.9 us (8%)
  waiting for transfers between devices  8.16 us (6%)
    all_to_all x1, blocking collectives, per_device(): b1 = lax.all_to_all(a1, ('zl', 'x', 'zh', 'k'), 0, 0, tiled=True)  27.4 us
    all_to_all x1, blocking collectives, per_device(): mine = lax.all_to_all(spread, 'x', 0, 0, tiled=True).reshape(AUX // 2, COLS)  24.3 us
    all_to_all x1, blocking collectives, per_device(): b2 = lax.all_to_all(a2, ('y', 'zl'), 0, 0, tiled=True)  16.1 us
    all_gather x1, blocking collectives, per_device(): second = lax.all_gather(second, 'zh', axis=0, tiled=True)  14.4 us
    pallas_call x9, Pallas kernels, call(): pl.pallas_call(kernel, out_shape=out_shape, in_specs=kinds, out_specs=jax...  11.9 us
    all_to_all x1, blocking collectives, per_device(): energy = lax.all_to_all(energy, ('zl', 'zh'), 0, 0, tiled=True)  9.87 us
    ppermute x1, starting transfers between devices, per_device(): other = lax.ppermute(mine, 'k', [(0, 1), (1, 0)])  7.66 us
    all_to_all x1, waiting for transfers between devices, per_device(): energy = lax.all_to_all(energy, ('y', 'x', 'k'), 0, 0, tiled=True)  7.31 us
  transfers between devices with their start and end apart: 3, of which 2 were waited for; matrix products, arithmetic and copies ran while one was open for 0% of the time, Pallas kernels for 4%

profile of v3, /device:TPU:1, one launch (start us, length us, event | category | flops | bytes accessed | tf_op | source)
XLA Modules:
  0.0 141.2 jit_solution(12652263108462588690)
XLA Ops:
  7.2 0.0 all-gather.2.cloned.1.call-start
  7.2 0.9 copy-done.2
  8.1 0.2 shard_map.68
  8.3 27.4 %all_to_all.25.in_ref = bf16[64,16,128]{2,1,0:T(8,128)(2,1)S(1)} all-to-all(bf16[64,16,128]{2,1,0:T(8,128)(2,1)S(1)} %get-tuple-element.10), channel_id=1, replica_groups=mesh['y'=8,'zl'=2,'x'=4,'zh'=4,'k'=2] {'zl','x','zh','k'}, dimensions={0} | all-to-all | bytes 524288 | tf_op jit(solution)/shard_map/all_to_all | solution.py:200
  35.7 0.8 shard_map.69
  36.6 0.0 all-gather.2.cloned.1.call-update
  36.6 16.1 %all_to_all.26.in_ref = bf16[16,32,128]{2,1,0:T(8,128)(2,1)S(1)} all-to-all(bf16[16,32,128]{2,1,0:T(8,128)(2,1)S(1)} %get-tuple-element.11), channel_id=1, replica_groups=mesh['y'=8,'zl'=2,'x'=4,'zh'=4,'k'=2] {'y','zl'}, dimensions={0} | all-to-all | bytes 262144 | tf_op jit(solution)/shard_map/all_to_all | solution.py:204
  52.7 0.1 shard_map.70
  52.9 14.4 %all_gather.6 = bf16[256,1024]{1,0:T(8,128)(2,1)S(1)} all-gather(bf16[64,1024]{1,0:T(8,128)(2,1)S(1)} %shard_map.70), channel_id=1, replica_groups=mesh['y'=8,'zl'=2,'x'=4,'zh'=4,'k'=2] {'zh'}, dimensions={0}, use_global_device_ids=true | all-gather | bytes 655360 | tf_op jit(solution)/shard_map/all_gather | solution.py:206
  67.3 0.3 broadcast_in_dim.2
  67.6 0.0 copy-start.3
  67.6 0.0 copy-start.4
  67.6 24.3 %all_to_all.27 = bf16[4,256,1024]{2,1,0:T(8,128)(2,1)S(1)} all-to-all(bf16[4,256,1024]{2,1,0:T(8,128)(2,1)S(1)} %broadcast_in_dim.2), channel_id=1, replica_groups=mesh['y'=8,'zl'=2,'x'=4,'zh'=4,'k'=2] {'x'}, dimensions={0} | all-to-all | bytes 4194304 | tf_op jit(solution)/shard_map/all_to_all | solution.py:208
  91.9 7.7 %collective-permute-start = (bf16[1024,1024]{1,0:T(8,128)(2,1)S(1)}, bf16[1024,1024]{1,0:T(8,128)(2,1)S(1)}, u32[]{:S(2)}, u32[]{:S(2)}) collective-permute-start(bf16[1024,1024]{1,0:T(8,128)(2,1)S(1)} %bitcast.5), channel_id=1, source_target_pairs={{0,1},{1,0},{2,3},{3,2},{4,5},{5,4},{6,7},{7,6},{8,9},{9,8},{10,11... | collective-permute-start | bytes 6291464 | tf_op jit(solution)/shard_map/ppermute | solution.py:210
  99.6 1.1 shard_map.72.inv_ref
  100.7 1.8 %shard_map.71.half_ref = f32[512,1024]{1,0:T(8,128)S(1)} custom-call(bf16[512,2048]{1,0:T(8,128)(2,1)S(1)} %copy-done, bf16[1024,1024]{1,0:T(8,128)(2,1)S(1)} %bitcast.6), custom_call_target="tpu_custom_call" | custom-call | flops 1073741824 | bytes 2097152 | tf_op jit(solution)/shard_map/pallas_call | solution.py:182
  102.5 0.8 collective-permute-done.r_ref
  103.3 3.7 %shard_map.73 = (bf16[512,1024]{1,0:T(8,128)(2,1)S(1)}, f32[8,2,128]{2,1,0:T(2,128)S(1)}) custom-call(f32[512,1024]{1,0:T(8,128)S(1)} %shard_map.71.half_ref, bf16[512,2048]{1,0:T(8,128)(2,1)S(1)} %copy-done, bf16[1024,1024]{1,0:T(8,128)(2,1)S(1)} %collective-permute-done.r_ref, f32[512,1024]{1,0:T(8,128)S(1)} %shard_map.72.inv_ref), custom_call_target="tpu_custom_call" | custom-call | tf_op jit(solution)/shard_map/pallas_call | solution.py:182
  107.0 9.9 %all_to_all.28.in_ref = f32[8,2,128]{2,1,0:T(2,128)S(1)} all-to-all(f32[8,2,128]{2,1,0:T(2,128)S(1)} %get-tuple-element.15), channel_id=1, replica_groups=mesh['y'=8,'zl'=2,'x'=4,'zh'=4,'k'=2] {'zl','zh'}, dimensions={0} | all-to-all | bytes 16384 | tf_op jit(solution)/shard_map/all_to_all | solution.py:227
  116.8 0.6 shard_map.75
  117.5 5.9 %all-to-all-start.4 = ((f32[64,2,128]{2,1,0:T(2,128)}), f32[64,2,128]{2,1,0:T(2,128)S(1)}, u32[]{:S(2)}, u32[]{:S(2)}) async-start(f32[64,2,128]{2,1,0:T(2,128)} %shard_map.75), calls=%async_computation.4 | async-start | bytes 131072 | tf_op jit(solution)/shard_map/all_to_all | solution.py:229
  123.4 2.8 %shard_map.74 = bf16[512,1024]{1,0:T(8,128)(2,1)} custom-call(bf16[512,1024]{1,0:T(8,128)(2,1)S(1)} %get-tuple-element.14.t_ref, bf16[1024,1024]{1,0:T(8,128)(2,1)S(1)} %copy-done.1), custom_call_target="tpu_custom_call" | custom-call | flops 1073741824 | bytes 2097152 | tf_op jit(solution)/shard_map/pallas_call | solution.py:182
  126.2 7.3 %all-to-all-done.4.in_ref = f32[64,2,128]{2,1,0:T(2,128)S(1)} async-done(((f32[64,2,128]{2,1,0:T(2,128)}), f32[64,2,128]{2,1,0:T(2,128)S(1)}, u32[]{:S(2)}, u32[]{:S(2)}) %all-to-all-start.4) | async-done | bytes 65568 | tf_op jit(solution)/shard_map/all_to_all | solution.py:229
  133.5 0.8 shard_map.76
  (10 shorter events, 0.0 us)
Async XLA Ops:
  7.2 84.7 %all-gather.2.cloned.1.call-start = ((), (), s32[]{:S(2)}) async-start(), calls=%async_computation.5 | async-start | bytes 2359296 | tf_op jit(solution)/shard_map/all_gather | solution.py:202
  7.2 0.9 copy-start.2
  67.6 32.0 %copy-start.3 = (f32[1024]{0:T(1024)S(1)}, f32[1024]{0:T(1024)}, u32[]{:S(2)}) copy-start(f32[1024]{0:T(1024)} %param.7) | copy-start | bytes 12292
  67.6 32.0 %copy-start.4 = (f32[16]{0:T(128)S(1)}, f32[16]{0:T(128)}, u32[]{:S(2)}) copy-start(f32[16]{0:T(128)} %occ_ref.1) | copy-start | bytes 196
  67.6 32.0 %copy-start.5 = (s32[16]{0:T(128)S(1)}, s32[16]{0:T(128)}, u32[]{:S(2)}) copy-start(s32[16]{0:T(128)} %slot_ref.1) | copy-start | bytes 196
  91.9 8.8 %copy-start = (bf16[512,2048]{1,0:T(8,128)(2,1)S(1)}, bf16[512,2048]{1,0:T(8,128)(2,1)}, u32[]{:S(2)}) copy-start(bf16[512,2048]{1,0:T(8,128)(2,1)} %all-gather.2.cloned.1.call-done.l_ref) | copy-start | bytes 6291460
  91.9 11.4 %collective-permute-start = (bf16[1024,1024]{1,0:T(8,128)(2,1)S(1)}, bf16[1024,1024]{1,0:T(8,128)(2,1)S(1)}, u32[]{:S(2)}, u32[]{:S(2)}) collective-permute-start(bf16[1024,1024]{1,0:T(8,128)(2,1)S(1)} %bitcast.5), channel_id=1, source_target_pairs={{0,1},{1,0},{2,3},{3,2},{4,5},{5,4},{6,7},{7,6},{8,9},{9,8},{10,11... | collective-permute-start | bytes 6291464 | tf_op jit(solution)/shard_map/ppermute | solution.py:210
  103.3 20.1 %copy-start.1 = (bf16[1024,1024]{1,0:T(8,128)(2,1)S(1)}, bf16[1024,1024]{1,0:T(8,128)(2,1)}, u32[]{:S(2)}) copy-start(bf16[1024,1024]{1,0:T(8,128)(2,1)} %constant.2.clone.perm_ref) | copy-start | bytes 6291460
  117.5 16.0 %all-to-all-start.4 = ((f32[64,2,128]{2,1,0:T(2,128)}), f32[64,2,128]{2,1,0:T(2,128)S(1)}, u32[]{:S(2)}, u32[]{:S(2)}) async-start(f32[64,2,128]{2,1,0:T(2,128)} %shard_map.75), calls=%async_computation.4 | async-start | bytes 131072 | tf_op jit(solution)/shard_map/all_to_all | solution.py:229
Sparse Core Ops, SparseCore 0:
  36.7 36.8 all-gather.1

commit v4 on v3

--- a/solution.py
+++ b/solution.py
@@ -101,30 +101,44 @@
 
 
 def main_kernel(half_ref, l_ref, r_ref, inv_ref, amp_ref, energy_ref, x_ref, z_ref):
-    @pl.loop(0, COLS // STEP)
-    def _(n):
-        lanes = pl.ds(pl.multiple_of(n * STEP, STEP), STEP)
+    low = low_half(WA)
+    tiles = COLS // 128
+    z_ref[...] = jnp.zeros_like(z_ref)
+
+    def at(i, tile):
+        return slice(i * WA, (i + 1) * WA), slice(tile * 128, (tile + 1) * 128)
+
+    def product(n):
+        lanes = slice(n * STEP, (n + 1) * STEP)
         x_ref[:, lanes] = half_ref[:, lanes] + jnp.dot(l_ref[:, AUX // 2 :], r_ref[:, lanes], preferred_element_type=jnp.float32)
 
-    low = low_half(WA)
-
-    @pl.loop(0, NOCC // 2)
-    def _(big_j):
-        lanes = pl.ds(pl.multiple_of(big_j * 128, 128), 128)
-        r0 = pl.multiple_of(big_j * 2 * WA, 2 * WA)
-        for big_i in range(NOCC // 2):
-            tile = slice(big_i * 128, (big_i + 1) * 128)
-            s0 = x_ref[pl.ds(r0, WA), tile]
-            s1 = x_ref[pl.ds(r0 + WA, WA), tile]
+    def ratios(big_i, big_j):
+        if big_i <= big_j:
+            s0 = x_ref[at(2 * big_j, big_i)]
+            s1 = x_ref[at(2 * big_j + 1, big_i)]
             swaps = (jnp.where(low, s0, pltpu.roll(s1, 64, 1)), jnp.where(low, pltpu.roll(s0, 64, 1), s1))
-            for e in range(2):
-                i = 2 * big_i + e
-                rows = slice(i * WA, (i + 1) * WA)
-                value = x_ref[rows, lanes]
-                ratio = value * inv_ref[rows, lanes]
-                amp_ref[rows, lanes] = ratio.astype(jnp.bfloat16)
+        for e in range(2):
+            i = 2 * big_i + e
+            value = x_ref[at(i, big_j)]
+            ratio = value * inv_ref[at(i, big_j)]
+            amp_ref[at(i, big_j)] = ratio.astype(jnp.bfloat16)
+            if big_i <= big_j:
                 part = ratio * (2.0 * value - swaps[e])
-                z_ref[i * 8 : (i + 1) * 8, lanes] = jnp.sum(part.reshape(WA // 8, 8, 128), axis=0)
+                z_ref[i * 8 : (i + 1) * 8, big_j * 128 : (big_j + 1) * 128] = jnp.sum(part.reshape(WA // 8, 8, 128), axis=0)
+
+    def finish(n):
+        width = STEP // 128
+        for new in range(n * width, (n + 1) * width):
+            for old in range(new + 1):
+                ratios(old, new)
+                if old < new:
+                    ratios(new, old)
+
+    product(0)
+    for n in range(1, COLS // STEP):
+        product(n)
+        finish(n - 1)
+    finish(COLS // STEP - 1)
 
     source = lax.broadcasted_iota(jnp.int32, (COLS, 128), 0) // WB
     target = lax.broadcasted_iota(jnp.int32, (COLS, 128), 1) % NOCC
@@ -135,13 +149,13 @@
     kept = jnp.where(row == lane, by_pair, 0.0)
     halves = [jnp.sum(kept[h * 64 : (h + 1) * 64], axis=0, keepdims=True) for h in range(2)]
     energy = jnp.concatenate(halves, axis=0)
-    for z in range(ZL * ZH):
+    for z in range(ZL * ZH * K):
         energy_ref[z] = energy
 
 
 def middle_kernel(in_ref, out_ref):
     total = jnp.sum(in_ref[...], axis=0)
-    for n in range(Y * X * K):
+    for n in range(Y * X):
         out_ref[n] = total
 
 
@@ -154,14 +168,23 @@
     source = lax.broadcasted_iota(jnp.int32, (128, NOCC), 0) % NOCC
     target = lax.broadcasted_iota(jnp.int32, (128, NOCC), 1)
     chooser = jnp.where(source == target, 1.0, 0.0)
-    out_ref[...] = jnp.dot(kept, chooser, preferred_element_type=jnp.float32, precision=lax.Precision.HIGHEST)
-
-
-def order_kernel(t_ref, perm_ref, amp_ref):
-    @pl.loop(0, COLS // STEP)
-    def _(n):
-        lanes = pl.ds(pl.multiple_of(n * STEP, STEP), STEP)
-        amp_ref[:, lanes] = jnp.dot(t_ref[...], perm_ref[:, lanes], preferred_element_type=jnp.float32).astype(jnp.bfloat16)
+    exact = dict(preferred_element_type=jnp.float32, precision=lax.Precision.HIGHEST)
+    upper = jnp.dot(kept, chooser, **exact)
+    mirror = lax.dot_general(chooser, kept, (((0,), (1,)), ((), ())), **exact)
+    i = lax.broadcasted_iota(jnp.int32, (NOCC, NOCC), 0)
+    j = lax.broadcasted_iota(jnp.int32, (NOCC, NOCC), 1)
+    out_ref[...] = jnp.where(i <= j, upper, mirror)
+
+
+def order_kernel(t_ref, perm_ref, amp_ref, buf_ref, sems):
+    copies = []
+    for n in range(COLS // STEP):
+        lanes = slice(n * STEP, (n + 1) * STEP)
+        buf_ref[:, lanes] = jnp.dot(t_ref[...], perm_ref[:, lanes], preferred_element_type=jnp.float32).astype(jnp.bfloat16)
+        copies.append(pltpu.make_async_copy(buf_ref.at[:, lanes], amp_ref.at[:, lanes], sems.at[n]))
+        copies[-1].start()
+    for copy in copies:
+        copy.wait()
 
 
 def permutation():
@@ -176,14 +199,14 @@
     return jax.ShapeDtypeStruct(dims, dtype)
 
 
-def call(kernel, out_shape, operands, in_specs=None, scratch=(), flops=0):
+def call(kernel, out_shape, operands, in_specs=None, scratch=(), flops=0, out=VMEM):
     kinds = in_specs or [VMEM] * len(operands)
     cost = pl.CostEstimate(flops=flops, bytes_accessed=4 * ROWS * COLS, transcendentals=0) if flops else None
     return pl.pallas_call(
         kernel,
         out_shape=out_shape,
         in_specs=kinds,
-        out_specs=jax.tree.map(lambda _: VMEM, out_shape),
+        out_specs=jax.tree.map(lambda _: out, out_shape),
         scratch_shapes=scratch,
         compiler_params=PARAMS,
         cost_estimate=cost,
@@ -219,14 +242,21 @@
     half = call(half_kernel, shape((ROWS, COLS), f32), [left, mine], flops=ROWS * COLS * AUX)
     ratio, energy = call(
         main_kernel,
-        (shape((ROWS, COLS)), shape((ZL * ZH, 2, 128), f32)),
+        (shape((ROWS, COLS)), shape((ZL * ZH * K, 2, 128), f32)),
         [half, left, other, inverse],
         scratch=[pltpu.VMEM((ROWS, COLS), f32), pltpu.VMEM((NOCC * 8, COLS), f32)],
     )
-    amp = call(order_kernel, shape((ROWS, COLS)), [ratio, permutation()], flops=2 * ROWS * COLS * COLS)
-    energy = lax.all_to_all(energy, ("zl", "zh"), 0, 0, tiled=True)
-    energy = call(middle_kernel, shape((Y * X * K, 2, 128), f32), [energy])
-    energy = lax.all_to_all(energy, ("y", "x", "k"), 0, 0, tiled=True)
+    amp = call(
+        order_kernel,
+        shape((ROWS, COLS)),
+        [ratio, permutation()],
+        scratch=[pltpu.VMEM((ROWS, COLS), jnp.bfloat16), pltpu.SemaphoreType.DMA((COLS // STEP,))],
+        flops=2 * ROWS * COLS * COLS,
+        out=pl.BlockSpec(memory_space=pl.ANY),
+    )
+    energy = lax.all_to_all(energy, ("zl", "zh", "k"), 0, 0, tiled=True)
+    energy = call(middle_kernel, shape((Y * X, 2, 128), f32), [energy])
+    energy = lax.all_to_all(energy, ("y", "x"), 0, 0, tiled=True)
     return amp.reshape(NOCC, WA, COLS), call(last_kernel, shape((NOCC, NOCC), f32), [energy])
 
 

time: 142 us -> 138 us (0.972)
  Pallas kernels: 11.9 us -> 9.6 us
  starting transfers between devices: 13.6 us -> 11.5 us
  blocking collectives: 92.1 us -> 93.6 us
    pallas_call x9, Pallas kernels: 11.9 us -> 9.6 us  [call(): pl.pallas_call(kernel, out_shape=out_shape, in_specs=kinds, out_specs=jax...]
    all_to_all x1, starting transfers between devices: 5.92 us -> 3.8 us  [per_device(): energy = lax.all_to_all(energy, ('y', 'x'), 0, 0, tiled=True)]
    all_to_all x1, blocking collectives: 9.87 us -> 11.3 us  [per_device(): energy = lax.all_to_all(energy, ('zl', 'zh', 'k'), 0, 0, tiled=True)]
where the time goes in v4:
time: 138 us; the launch traced here: 137 us
  blocking collectives  93.6 us (68%)
  between operations  14.2 us (10%)
  starting transfers between devices  11.5 us (8%)
  Pallas kernels  9.6 us (7%)
  waiting for transfers between devices  7.35 us (5%)
    all_to_all x1, blocking collectives, per_device(): b1 = lax.all_to_all(a1, ('zl', 'x', 'zh', 'k'), 0, 0, tiled=True)  27.4 us
    all_to_all x1, blocking collectives, per_device(): mine = lax.all_to_all(spread, 'x', 0, 0, tiled=True).reshape(AUX // 2, COLS)  24.3 us
    all_to_all x1, blocking collectives, per_device(): b2 = lax.all_to_all(a2, ('y', 'zl'), 0, 0, tiled=True)  16.1 us
    all_gather x1, blocking collectives, per_device(): second = lax.all_gather(second, 'zh', axis=0, tiled=True)  14.4 us
    all_to_all x1, blocking collectives, per_device(): energy = lax.all_to_all(energy, ('zl', 'zh', 'k'), 0, 0, tiled=True)  11.3 us
    pallas_call x9, Pallas kernels, call(): pl.pallas_call(kernel, out_shape=out_shape, in_specs=kinds, out_specs=jax...  9.6 us
    ppermute x1, starting transfers between devices, per_device(): other = lax.ppermute(mine, 'k', [(0, 1), (1, 0)])  7.66 us
    all_to_all x1, waiting for transfers between devices, per_device(): energy = lax.all_to_all(energy, ('y', 'x'), 0, 0, tiled=True)  6.49 us
  transfers between devices with their start and end apart: 3, of which 2 were waited for; matrix products, arithmetic and copies ran while one was open for 0% of the time, Pallas kernels for 4%

profile of v4, /device:TPU:1, one launch (start us, length us, event | category | flops | bytes accessed | tf_op | source)
XLA Modules:
  0.0 137.4 jit_solution(16225397414338763339)
XLA Ops:
  7.2 0.0 all-gather.2.cloned.1.call-start
  7.2 0.9 copy-done.2
  8.1 0.2 shard_map.68
  8.3 27.4 %all_to_all.25.in_ref = bf16[64,16,128]{2,1,0:T(8,128)(2,1)S(1)} all-to-all(bf16[64,16,128]{2,1,0:T(8,128)(2,1)S(1)} %get-tuple-element.10), channel_id=1, replica_groups=mesh['y'=8,'zl'=2,'x'=4,'zh'=4,'k'=2] {'zl','x','zh','k'}, dimensions={0} | all-to-all | bytes 524288 | tf_op jit(solution)/shard_map/all_to_all | solution.py:223
  35.7 0.8 shard_map.69
  36.6 0.0 all-gather.2.cloned.1.call-update
  36.6 16.1 %all_to_all.26.in_ref = bf16[16,32,128]{2,1,0:T(8,128)(2,1)S(1)} all-to-all(bf16[16,32,128]{2,1,0:T(8,128)(2,1)S(1)} %get-tuple-element.11), channel_id=1, replica_groups=mesh['y'=8,'zl'=2,'x'=4,'zh'=4,'k'=2] {'y','zl'}, dimensions={0} | all-to-all | bytes 262144 | tf_op jit(solution)/shard_map/all_to_all | solution.py:227
  52.7 0.1 shard_map.70
  52.9 14.4 %all_gather.6 = bf16[256,1024]{1,0:T(8,128)(2,1)S(1)} all-gather(bf16[64,1024]{1,0:T(8,128)(2,1)S(1)} %shard_map.70), channel_id=1, replica_groups=mesh['y'=8,'zl'=2,'x'=4,'zh'=4,'k'=2] {'zh'}, dimensions={0}, use_global_device_ids=true | all-gather | bytes 655360 | tf_op jit(solution)/shard_map/all_gather | solution.py:229
  67.3 0.3 broadcast_in_dim.2
  67.6 0.0 copy-start.3
  67.6 0.0 copy-start.4
  67.6 24.3 %all_to_all.27 = bf16[4,256,1024]{2,1,0:T(8,128)(2,1)S(1)} all-to-all(bf16[4,256,1024]{2,1,0:T(8,128)(2,1)S(1)} %broadcast_in_dim.2), channel_id=1, replica_groups=mesh['y'=8,'zl'=2,'x'=4,'zh'=4,'k'=2] {'x'}, dimensions={0} | all-to-all | bytes 4194304 | tf_op jit(solution)/shard_map/all_to_all | solution.py:231
  91.9 7.7 %collective-permute-start = (bf16[1024,1024]{1,0:T(8,128)(2,1)S(1)}, bf16[1024,1024]{1,0:T(8,128)(2,1)S(1)}, u32[]{:S(2)}, u32[]{:S(2)}) collective-permute-start(bf16[1024,1024]{1,0:T(8,128)(2,1)S(1)} %bitcast.5), channel_id=1, source_target_pairs={{0,1},{1,0},{2,3},{3,2},{4,5},{5,4},{6,7},{7,6},{8,9},{9,8},{10,11... | collective-permute-start | bytes 6291464 | tf_op jit(solution)/shard_map/ppermute | solution.py:233
  99.6 1.1 shard_map.72.inv_ref
  100.7 1.8 %shard_map.71.half_ref = f32[512,1024]{1,0:T(8,128)S(1)} custom-call(bf16[512,2048]{1,0:T(8,128)(2,1)S(1)} %copy-done, bf16[1024,1024]{1,0:T(8,128)(2,1)S(1)} %bitcast.6), custom_call_target="tpu_custom_call" | custom-call | flops 1073741824 | bytes 2097152 | tf_op jit(solution)/shard_map/pallas_call | solution.py:205
  102.5 0.8 collective-permute-done.r_ref
  103.3 2.0 %shard_map.73 = (bf16[512,1024]{1,0:T(8,128)(2,1)S(1)}, f32[16,2,128]{2,1,0:T(2,128)S(1)}) custom-call(f32[512,1024]{1,0:T(8,128)S(1)} %shard_map.71.half_ref, bf16[512,2048]{1,0:T(8,128)(2,1)S(1)} %copy-done, bf16[1024,1024]{1,0:T(8,128)(2,1)S(1)} %collective-permute-done.r_ref, f32[512,1024]{1,0:T(8,128)S(1)} %shard_map.72.inv_ref), custom_call_target="tpu_custom_call" | custom-call | tf_op jit(solution)/shard_map/pallas_call | solution.py:205
  105.3 11.3 %all_to_all.28.in_ref = f32[16,2,128]{2,1,0:T(2,128)S(1)} all-to-all(f32[16,2,128]{2,1,0:T(2,128)S(1)} %get-tuple-element.15), channel_id=1, replica_groups=mesh['y'=8,'zl'=2,'x'=4,'zh'=4,'k'=2] {'zl','zh','k'}, dimensions={0} | all-to-all | bytes 32768 | tf_op jit(solution)/shard_map/all_to_all | solution.py:257
  116.6 0.6 shard_map.75
  117.3 3.8 %all-to-all-start.4 = ((f32[32,2,128]{2,1,0:T(2,128)}), f32[32,2,128]{2,1,0:T(2,128)S(1)}, u32[]{:S(2)}, u32[]{:S(2)}) async-start(f32[32,2,128]{2,1,0:T(2,128)} %shard_map.75), calls=%async_computation.4 | async-start | bytes 65536 | tf_op jit(solution)/shard_map/all_to_all | solution.py:259
  121.1 2.1 %shard_map.74 = bf16[512,1024]{1,0:T(8,128)(2,1)} custom-call(bf16[512,1024]{1,0:T(8,128)(2,1)S(1)} %get-tuple-element.14.t_ref, bf16[1024,1024]{1,0:T(8,128)(2,1)S(1)} %copy-done.1), custom_call_target="tpu_custom_call" | custom-call | flops 1073741824 | bytes 2097152 | tf_op jit(solution)/shard_map/pallas_call | solution.py:205
  123.2 6.5 %all-to-all-done.4.in_ref = f32[32,2,128]{2,1,0:T(2,128)S(1)} async-done(((f32[32,2,128]{2,1,0:T(2,128)}), f32[32,2,128]{2,1,0:T(2,128)S(1)}, u32[]{:S(2)}, u32[]{:S(2)}) %all-to-all-start.4) | async-done | bytes 32800 | tf_op jit(solution)/shard_map/all_to_all | solution.py:259
  129.7 0.8 shard_map.76
  (10 shorter events, 0.0 us)
Async XLA Ops:
  7.2 84.7 %all-gather.2.cloned.1.call-start = ((), (), s32[]{:S(2)}) async-start(), calls=%async_computation.5 | async-start | bytes 2359296 | tf_op jit(solution)/shard_map/all_gather | solution.py:225
  7.2 0.9 copy-start.2
  67.6 32.0 %copy-start.3 = (f32[1024]{0:T(1024)S(1)}, f32[1024]{0:T(1024)}, u32[]{:S(2)}) copy-start(f32[1024]{0:T(1024)} %param.7) | copy-start | bytes 12292
  67.6 32.0 %copy-start.4 = (f32[16]{0:T(128)S(1)}, f32[16]{0:T(128)}, u32[]{:S(2)}) copy-start(f32[16]{0:T(128)} %occ_ref.1) | copy-start | bytes 196
  67.6 32.0 %copy-start.5 = (s32[16]{0:T(128)S(1)}, s32[16]{0:T(128)}, u32[]{:S(2)}) copy-start(s32[16]{0:T(128)} %slot_ref.1) | copy-start | bytes 196
  91.9 8.8 %copy-start = (bf16[512,2048]{1,0:T(8,128)(2,1)S(1)}, bf16[512,2048]{1,0:T(8,128)(2,1)}, u32[]{:S(2)}) copy-start(bf16[512,2048]{1,0:T(8,128)(2,1)} %all-gather.2.cloned.1.call-done.l_ref) | copy-start | bytes 6291460
  91.9 11.4 %collective-permute-start = (bf16[1024,1024]{1,0:T(8,128)(2,1)S(1)}, bf16[1024,1024]{1,0:T(8,128)(2,1)S(1)}, u32[]{:S(2)}, u32[]{:S(2)}) collective-permute-start(bf16[1024,1024]{1,0:T(8,128)(2,1)S(1)} %bitcast.5), channel_id=1, source_target_pairs={{0,1},{1,0},{2,3},{3,2},{4,5},{5,4},{6,7},{7,6},{8,9},{9,8},{10,11... | collective-permute-start | bytes 6291464 | tf_op jit(solution)/shard_map/ppermute | solution.py:233
  103.3 17.8 %copy-start.1 = (bf16[1024,1024]{1,0:T(8,128)(2,1)S(1)}, bf16[1024,1024]{1,0:T(8,128)(2,1)}, u32[]{:S(2)}) copy-start(bf16[1024,1024]{1,0:T(8,128)(2,1)} %constant.2.clone.perm_ref) | copy-start | bytes 6291460
  117.3 12.4 %all-to-all-start.4 = ((f32[32,2,128]{2,1,0:T(2,128)}), f32[32,2,128]{2,1,0:T(2,128)S(1)}, u32[]{:S(2)}, u32[]{:S(2)}) async-start(f32[32,2,128]{2,1,0:T(2,128)} %shard_map.75), calls=%async_computation.4 | async-start | bytes 65536 | tf_op jit(solution)/shard_map/all_to_all | solution.py:259
Sparse Core Ops, SparseCore 0:
  36.7 36.8 all-gather.1

commit v5 on v4

--- a/solution.py
+++ b/solution.py
@@ -14,9 +14,12 @@
 WB = NV // GRP
 ROWS, COLS = NOCC * WA, NOCC * WB
 STEP = 256
+CHUNK = ZH * PB
+ARRIVAL = tuple((d, rel) for d in (0, 1, 3, 2) for rel in range(K))
+GROUP = 2 * CHUNK
 VMEM = pl.BlockSpec(memory_space=pltpu.VMEM)
 SMEM = pl.BlockSpec(memory_space=pltpu.SMEM)
-PARAMS = pltpu.CompilerParams(vmem_limit_bytes=16 * 1024 * 1024)
+ANY = pl.BlockSpec(memory_space=pl.ANY)
 
 
 def low_half(rows):
@@ -43,25 +46,31 @@
             bottom = both[s * WA + WA // 2 : (s + 1) * WA]
             piece = jnp.where(low, top, bottom).astype(jnp.bfloat16)
             c = t * (128 // WA) + s
-            for z in range(ZL):
-                a1_ref[z * COL + c] = piece
+            a1_ref[c] = piece
         even, odd = pair_halves(tile[: PB // 2], tile[PB // 2 :])
         a2_ref[2 * t] = even
         a2_ref[2 * t + 1] = odd
 
 
 def first_kernel(in_ref, out_ref):
-    own = lax.axis_index("k")
-    for z in range(ZL):
-        for rel in range(K):
-            k = own if rel == 0 else 1 - own
-            for x in range(X):
-                for m in range(ZH // 2):
-                    base = z * COL + (x * ZH + 2 * m) * K
-                    top, bottom = pair_halves(in_ref[base + k], in_ref[base + K + k])
-                    lanes = ((rel * X + x) * ZH + 2 * m) * PB
-                    out_ref[z, 0 : WA // 2, lanes : lanes + 128] = top
-                    out_ref[z, WA // 2 : WA, lanes : lanes + 128] = bottom
+    own_k, own_x = lax.axis_index("k"), lax.axis_index("x")
+    for n, (d, rel) in enumerate(ARRIVAL):
+        k = (own_k + rel) % K
+        x = (own_x + X - d) % X
+        for m in range(ZH // 2):
+            base = (x * ZH + 2 * m) * K + k
+            top, bottom = pair_halves(in_ref[base], in_ref[base + K])
+            lanes = (n * ZH + 2 * m) * PB
+            for y in range(Y):
+                out_ref[y, 0 : WA // 2, lanes : lanes + 128] = top
+                out_ref[y, WA // 2 : WA, lanes : lanes + 128] = bottom
+
+
+def place_kernel(own_ref, near_ref, out_ref):
+    zl = lax.axis_index("zl")
+    for y in range(Y):
+        out_ref[y, zl] = own_ref[y]
+        out_ref[y, 1 - zl] = near_ref[y]
 
 
 def second_kernel(in_ref, out_ref):
@@ -93,24 +102,43 @@
             inv_ref[i * WA : (i + 1) * WA, lanes] = 1.0 / (second + occ_ref[slot_ref[i]])
 
 
-def half_kernel(l_ref, r_ref, x_ref):
-    @pl.loop(0, COLS // STEP)
-    def _(n):
-        lanes = pl.ds(pl.multiple_of(n * STEP, STEP), STEP)
-        x_ref[:, lanes] = jnp.dot(l_ref[:, : AUX // 2], r_ref[:, lanes], preferred_element_type=jnp.float32)
-
-
-def main_kernel(half_ref, l_ref, r_ref, inv_ref, amp_ref, energy_ref, x_ref, z_ref):
+def levels_kernel(occ_ref, slot_ref, vir_ref, out_ref, v_ref):
+    column = (lax.axis_index("x") * ZH + lax.axis_index("zh")) * K + lax.axis_index("k")
+    group = lax.axis_index("y") * ZL + lax.axis_index("zl")
+    first_row = vir_ref[pl.ds(column // 4, 1), :]
+    v_ref[...] = jnp.broadcast_to(first_row, (128, 128)).T
+    first = v_ref[pl.ds(pl.multiple_of((column % 4) * WA, WA), WA), :]
+    second_row = vir_ref[pl.ds(group // 2, 1), :]
+    low1 = lax.broadcasted_iota(jnp.int32, (1, 128), 1) < 64
+    swapped_row = pltpu.roll(jnp.broadcast_to(second_row, (8, 128)), 64, 1)[:1]
+    odd = group % 2 == 1
+    v_second = jnp.where(low1 != odd, second_row, swapped_row)
+    for t in range(NOCC // 2):
+        occ = jnp.where(low1, occ_ref[slot_ref[2 * t]], occ_ref[slot_ref[2 * t + 1]])
+        out_ref[:WA, t * 128 : (t + 1) * 128] = occ - v_second - first
+    for i in range(NOCC):
+        out_ref[WA + i : WA + i + 1, :128] = jnp.broadcast_to(occ_ref[slot_ref[i]], (1, 128))
+
+
+def main_kernel(l_ref, levels_ref, *refs):
+    blocks, (amp_ref, energy_ref, x_ref, z_ref) = refs[:-4], refs[-4:]
+    starts = [sum(ref.shape[0] for ref in blocks[:n]) for n in range(len(blocks))]
+    groups = AUX // GROUP
     low = low_half(WA)
-    tiles = COLS // 128
     z_ref[...] = jnp.zeros_like(z_ref)
 
     def at(i, tile):
         return slice(i * WA, (i + 1) * WA), slice(tile * 128, (tile + 1) * 128)
 
-    def product(n):
+    def product(n, g=groups - 1):
         lanes = slice(n * STEP, (n + 1) * STEP)
-        x_ref[:, lanes] = half_ref[:, lanes] + jnp.dot(l_ref[:, AUX // 2 :], r_ref[:, lanes], preferred_element_type=jnp.float32)
+        parts = []
+        for start, ref in zip(starts, blocks):
+            if start // GROUP == g:
+                inner = slice(start, start + ref.shape[0])
+                parts.append(jnp.dot(l_ref[:, inner], ref[:, lanes], preferred_element_type=jnp.float32))
+        total = sum(parts[1:], parts[0])
+        x_ref[:, lanes] = total if g == 0 else x_ref[:, lanes] + total
 
     def ratios(big_i, big_j):
         if big_i <= big_j:
@@ -120,7 +148,7 @@
         for e in range(2):
             i = 2 * big_i + e
             value = x_ref[at(i, big_j)]
-            ratio = value * inv_ref[at(i, big_j)]
+            ratio = value / (levels_ref[:WA, big_j * 128 : (big_j + 1) * 128] + levels_ref[WA + i : WA + i + 1, :128])
             amp_ref[at(i, big_j)] = ratio.astype(jnp.bfloat16)
             if big_i <= big_j:
                 part = ratio * (2.0 * value - swaps[e])
@@ -134,7 +162,9 @@
                 if old < new:
                     ratios(new, old)
 
-    product(0)
+    for g in range(groups):
+        for n in range(COLS // STEP if g < groups - 1 else 1):
+            product(n, g)
     for n in range(1, COLS // STEP):
         product(n)
         finish(n - 1)
@@ -176,30 +206,30 @@
     out_ref[...] = jnp.where(i <= j, upper, mirror)
 
 
-def order_kernel(t_ref, perm_ref, amp_ref, buf_ref, sems):
+def order_kernel(t_hbm, amp_ref, buf_ref, t_ref, sems):
+    load = pltpu.make_async_copy(t_hbm, t_ref, sems.at[COLS // STEP])
+    load.start()
+    row = lax.broadcasted_iota(jnp.int32, (COLS, STEP), 0)
+    lane = lax.broadcasted_iota(jnp.int32, (COLS, STEP), 1)
     copies = []
     for n in range(COLS // STEP):
         lanes = slice(n * STEP, (n + 1) * STEP)
-        buf_ref[:, lanes] = jnp.dot(t_ref[...], perm_ref[:, lanes], preferred_element_type=jnp.float32).astype(jnp.bfloat16)
+        source = (lane % NOCC) * WB + lane // NOCC + n * (STEP // NOCC)
+        chooser = jnp.where(row == source, 1.0, 0.0).astype(jnp.bfloat16)
+        if n == 0:
+            load.wait()
+        buf_ref[:, lanes] = jnp.dot(t_ref[...], chooser, preferred_element_type=jnp.float32).astype(jnp.bfloat16)
         copies.append(pltpu.make_async_copy(buf_ref.at[:, lanes], amp_ref.at[:, lanes], sems.at[n]))
         copies[-1].start()
     for copy in copies:
         copy.wait()
 
 
-def permutation():
-    source = np.arange(COLS)
-    target = (source % WB) * NOCC + source // WB
-    matrix = np.zeros((COLS, COLS), np.float32)
-    matrix[source, target] = 1.0
-    return jnp.asarray(matrix, jnp.bfloat16)
-
-
 def shape(dims, dtype=jnp.bfloat16):
     return jax.ShapeDtypeStruct(dims, dtype)
 
 
-def call(kernel, out_shape, operands, in_specs=None, scratch=(), flops=0, out=VMEM):
+def call(kernel, out_shape, operands, in_specs=None, scratch=(), flops=0, out=VMEM, limit=16):
     kinds = in_specs or [VMEM] * len(operands)
     cost = pl.CostEstimate(flops=flops, bytes_accessed=4 * ROWS * COLS, transcendentals=0) if flops else None
     return pl.pallas_call(
@@ -208,52 +238,67 @@
         in_specs=kinds,
         out_specs=jax.tree.map(lambda _: out, out_shape),
         scratch_shapes=scratch,
-        compiler_params=PARAMS,
+        compiler_params=pltpu.CompilerParams(vmem_limit_bytes=limit * 1024 * 1024),
         cost_estimate=cost,
     )(*operands)
+
+
+def run_main(left, levels, blocks):
+    f32 = jnp.float32
+    return call(
+        main_kernel,
+        (shape((ROWS, COLS)), shape((ZL * ZH * K, 2, 128), f32)),
+        [left, levels] + blocks,
+        scratch=[pltpu.VMEM((ROWS, COLS), f32), pltpu.VMEM((NOCC * 8, COLS), f32)],
+    )
+
+
+def run_order(ratio):
+    return call(
+        order_kernel,
+        shape((ROWS, COLS)),
+        [ratio],
+        scratch=[pltpu.VMEM((ROWS, COLS), jnp.bfloat16), pltpu.VMEM((ROWS, COLS), jnp.bfloat16), pltpu.SemaphoreType.DMA((COLS // STEP + 1,))],
+        in_specs=[ANY],
+        limit=62,
+        flops=2 * ROWS * COLS * COLS,
+        out=ANY,
+    )
 
 
 def per_device(factors, occ_levels, vir_levels, slot_orbital):
     f32 = jnp.float32
     a1, a2 = call(
         prep_kernel,
-        (shape((ZL * COL, WA // 2, 128)), shape((GRP, PB // 2, 128))),
+        (shape((COL, WA // 2, 128)), shape((GRP, PB // 2, 128))),
         [factors.reshape(PB, NV)],
     )
-    b1 = lax.all_to_all(a1, ("zl", "x", "zh", "k"), 0, 0, tiled=True)
-    first = call(first_kernel, shape((ZL, WA, AUX)), [b1])
-    left = lax.all_gather(first.reshape(ZL * WA, AUX), "y", axis=0, tiled=True)
+    b1 = lax.all_to_all(a1, ("x", "zh", "k"), 0, 0, tiled=True)
+    first = call(first_kernel, shape((Y, WA, AUX)), [b1])
     a2, _ = lax.optimization_barrier((a2, first))
     b2 = lax.all_to_all(a2, ("y", "zl"), 0, 0, tiled=True)
+    first, b2 = lax.optimization_barrier((first, b2))
+    own = lax.all_to_all(first, "y", 0, 0, tiled=True)
     second = call(second_kernel, shape((PB, COLS)), [b2])
     second = lax.all_gather(second, "zh", axis=0, tiled=True)
-    spread = jnp.broadcast_to(second[None], (X, ZH * PB, COLS))
-    mine = lax.all_to_all(spread, "x", 0, 0, tiled=True).reshape(AUX // 2, COLS)
-    mine, left = lax.optimization_barrier((mine, left))
-    other = lax.ppermute(mine, "k", [(0, 1), (1, 0)])
-    inverse = call(
-        inverse_kernel,
-        shape((ROWS, COLS), f32),
+    near = lax.ppermute(own, "zl", [(0, 1), (1, 0)])
+    up, down = [(i, (i + 1) % X) for i in range(X)], [(i, (i - 1) % X) for i in range(X)]
+    below, above = lax.ppermute(second, "x", up), lax.ppermute(second, "x", down)
+    second, own = lax.optimization_barrier((second, own))
+    far = [lax.ppermute(below[: CHUNK // 2], "x", up), lax.ppermute(above[CHUNK // 2 :], "x", down)]
+    mine = [second, below, above, jnp.concatenate(far, axis=0)]
+    other = [lax.ppermute(block, "k", [(0, 1), (1, 0)]) for block in mine]
+    blocks = [side[n] for n in range(4) for side in (mine, other)]
+    left = call(place_kernel, shape((Y, ZL, WA, AUX)), [own, near]).reshape(ROWS, AUX)
+    levels = call(
+        levels_kernel,
+        shape((WA + NOCC, COLS), f32),
         [occ_levels, slot_orbital, vir_levels.reshape(8, 128)],
         in_specs=[SMEM, SMEM, VMEM],
-        scratch=[pltpu.VMEM((WA, 128), f32), pltpu.VMEM((128, 128), f32)],
-        flops=ROWS * COLS * 10,
-    )
-    half = call(half_kernel, shape((ROWS, COLS), f32), [left, mine], flops=ROWS * COLS * AUX)
-    ratio, energy = call(
-        main_kernel,
-        (shape((ROWS, COLS)), shape((ZL * ZH * K, 2, 128), f32)),
-        [half, left, other, inverse],
-        scratch=[pltpu.VMEM((ROWS, COLS), f32), pltpu.VMEM((NOCC * 8, COLS), f32)],
-    )
-    amp = call(
-        order_kernel,
-        shape((ROWS, COLS)),
-        [ratio, permutation()],
-        scratch=[pltpu.VMEM((ROWS, COLS), jnp.bfloat16), pltpu.SemaphoreType.DMA((COLS // STEP,))],
-        flops=2 * ROWS * COLS * COLS,
-        out=pl.BlockSpec(memory_space=pl.ANY),
-    )
+        scratch=[pltpu.VMEM((128, 128), f32)],
+    )
+    ratio, energy = run_main(left, levels, blocks)
+    amp = run_order(ratio)
     energy = lax.all_to_all(energy, ("zl", "zh", "k"), 0, 0, tiled=True)
     energy = call(middle_kernel, shape((Y * X, 2, 128), f32), [energy])
     energy = lax.all_to_all(energy, ("y", "x"), 0, 0, tiled=True)

time: 138 us -> 133 us (0.964)
  blocking collectives: 93.6 us -> 66.1 us
  starting transfers between devices: 11.5 us -> 32.9 us
  between operations: 14.2 us -> 0.89 us
  waiting for transfers between devices: 7.35 us -> 20.6 us
    all_to_all x2 -> x1, blocking collectives: 51.7 us -> 25.6 us  [per_device(): b1 = lax.all_to_all(a1, ('x', 'zh', 'k'), 0, 0, tiled=True)]
    ppermute x1 -> x9, starting transfers between devices: 7.66 us -> 25.4 us  [the longest x4 10.3 us: per_device(): other = [lax.ppermute(block, 'k', [(0, 1), (1, 0)]) for block in mine]]
    all_to_all x0 -> x1, waiting for transfers between devices: none -> 8.94 us  [per_device(): own = lax.all_to_all(first, 'y', 0, 0, tiled=True)]
    ppermute x1 -> x9, waiting for transfers between devices: 0.84 us -> 6.3 us  [the longest x1 6.28 us: per_device(): near = lax.ppermute(own, 'zl', [(0, 1), (1, 0)])]
    all_to_all x0 -> x1, starting transfers between devices: none -> 3.69 us  [per_device(): own = lax.all_to_all(first, 'y', 0, 0, tiled=True)]
  transfers between devices with their start and end apart: 3 -> 11, of which waited for: 2 -> 3; matrix products, arithmetic and copies ran while one was open for 0% -> 0% of each run, Pallas kernels for 4% -> 3%
where the time goes in v5:
time: 133 us
  blocking collectives  66.1 us (50%)
  starting transfers between devices  32.9 us (25%)
  waiting for transfers between devices  20.6 us (15%)
  Pallas kernels  10.3 us (8%)
  local copies, waits for them, and re-layouts  1.96 us (1%)
    all_to_all x1, blocking collectives, per_device(): b1 = lax.all_to_all(a1, ('x', 'zh', 'k'), 0, 0, tiled=True)  25.6 us
    all_to_all x1, blocking collectives, per_device(): b2 = lax.all_to_all(a2, ('y', 'zl'), 0, 0, tiled=True)  15.9 us
    all_gather x1, blocking collectives, per_device(): second = lax.all_gather(second, 'zh', axis=0, tiled=True)  13.6 us
    all_to_all x1, blocking collectives, per_device(): energy = lax.all_to_all(energy, ('zl', 'zh', 'k'), 0, 0, tiled=True)  11.1 us
    pallas_call x9, Pallas kernels, call(): pl.pallas_call(kernel, out_shape=out_shape, in_specs=kinds, out_specs=jax...  10.3 us
    ppermute x4, starting transfers between devices, per_device(): other = [lax.ppermute(block, 'k', [(0, 1), (1, 0)]) for block in mine]  10.3 us
    all_to_all x1, waiting for transfers between devices, per_device(): own = lax.all_to_all(first, 'y', 0, 0, tiled=True)  8.94 us
    ppermute x1, waiting for transfers between devices, per_device(): near = lax.ppermute(own, 'zl', [(0, 1), (1, 0)])  6.28 us
  transfers between devices with their start and end apart: 11, of which 3 were waited for; matrix products, arithmetic and copies ran while one was open for 0% of the time, Pallas kernels for 3%

profile of v5, /device:TPU:1, one launch (start us, length us, event | category | flops | bytes accessed | tf_op | source)
XLA Modules:
  0.0 132.8 jit_solution(1305547670462407449)
XLA Ops:
  0.6 0.9 copy-done
  1.7 25.6 %all_to_all.25.in_ref = bf16[32,16,128]{2,1,0:T(8,128)(2,1)S(1)} all-to-all(bf16[32,16,128]{2,1,0:T(8,128)(2,1)S(1)} %get-tuple-element.11), channel_id=1, replica_groups=mesh['y'=8,'zl'=2,'x'=4,'zh'=4,'k'=2] {'x','zh','k'}, dimensions={0} | all-to-all | bytes 262144 | tf_op jit(solution)/shard_map/all_to_all | solution.py:276
  27.3 1.3 shard_map.60
  28.6 15.9 %all_to_all.26.in_ref = bf16[16,32,128]{2,1,0:T(8,128)(2,1)S(1)} all-to-all(bf16[16,32,128]{2,1,0:T(8,128)(2,1)S(1)} %get-tuple-element.13), channel_id=1, replica_groups=mesh['y'=8,'zl'=2,'x'=4,'zh'=4,'k'=2] {'y','zl'}, dimensions={0} | all-to-all | bytes 262144 | tf_op jit(solution)/shard_map/all_to_all | solution.py:279
  44.5 3.7 %all-to-all-start.2 = ((bf16[8,32,2048]{2,1,0:T(8,128)(2,1)}), bf16[8,32,2048]{2,1,0:T(8,128)(2,1)S(1)}, u32[]{:S(2)}, u32[]{:S(2)}) async-start(bf16[8,32,2048]{2,1,0:T(8,128)(2,1)} %shard_map.60), calls=%async_computation.2 | async-start | bytes 2097152 | tf_op jit(solution)/shard_map/all_to_all | solution.py:281
  48.3 13.6 %all_gather.3.refs_0_ = bf16[256,1024]{1,0:T(8,128)(2,1)S(1)} all-gather(bf16[64,1024]{1,0:T(8,128)(2,1)S(1)} %shard_map.61), channel_id=1, replica_groups=mesh['y'=8,'zl'=2,'x'=4,'zh'=4,'k'=2] {'zh'}, dimensions={0}, use_global_device_ids=true | all-gather | bytes 655360 | tf_op jit(solution)/shard_map/all_gather | solution.py:283
  61.9 2.5 %collective-permute-start.2 = (bf16[256,1024]{1,0:T(8,128)(2,1)S(1)}, bf16[256,1024]{1,0:T(8,128)(2,1)S(1)}, u32[]{:S(2)}, u32[]{:S(2)}) collective-permute-start(bf16[256,1024]{1,0:T(8,128)(2,1)S(1)} %all_gather.3.refs_0_), channel_id=1, source_target_pairs={{0,8},{8,16},{16,24},{24,0},{1,9},{9,17},{17,25},{25,1},{2,10},{10... | collective-permute-start | bytes 1572872 | tf_op jit(solution)/shard_map/ppermute | solution.py:286
  64.3 4.0 %collective-permute-start.4 = (bf16[256,1024]{1,0:T(8,128)(2,1)S(1)}, bf16[256,1024]{1,0:T(8,128)(2,1)S(1)}, u32[]{:S(2)}, u32[]{:S(2)}) collective-permute-start(bf16[256,1024]{1,0:T(8,128)(2,1)S(1)} %all_gather.3.refs_0_), channel_id=1, source_target_pairs={{0,24},{8,0},{16,8},{24,16},{1,25},{9,1},{17,9},{25,17},{2,26},{10... | collective-permute-start | bytes 1572872 | tf_op jit(solution)/shard_map/ppermute | solution.py:286
  68.4 8.9 %all-to-all-done.2.own_ref = bf16[8,32,2048]{2,1,0:T(8,128)(2,1)S(1)} async-done(((bf16[8,32,2048]{2,1,0:T(8,128)(2,1)}), bf16[8,32,2048]{2,1,0:T(8,128)(2,1)S(1)}, u32[]{:S(2)}, u32[]{:S(2)}) %all-to-all-start.2) | async-done | bytes 1048608 | tf_op jit(solution)/shard_map/all_to_all | solution.py:281
  77.3 2.2 %collective-permute-start = (bf16[8,32,2048]{2,1,0:T(8,128)(2,1)S(1)}, bf16[8,32,2048]{2,1,0:T(8,128)(2,1)S(1)}, u32[]{:S(2)}, u32[]{:S(2)}) collective-permute-start(bf16[8,32,2048]{2,1,0:T(8,128)(2,1)S(1)} %all-to-all-done.2.own_ref), channel_id=1, source_target_pairs={{0,32},{32,0},{1,33},{33,1},{2,34},{34,2},{3,35},{35,3},{4,36},{36... | collective-permute-start | bytes 3145736 | tf_op jit(solution)/shard_map/ppermute | solution.py:284
  79.5 2.3 %collective-permute-start.6 = (bf16[128,1024]{1,0:T(8,128)(2,1)S(1)}, bf16[128,1024]{1,0:T(8,128)(2,1)S(1)}, u32[]{:S(2)}, u32[]{:S(2)}) collective-permute-start(bf16[128,1024]{1,0:T(8,128)(2,1)S(1)} %slice.8), channel_id=1, source_target_pairs={{0,8},{8,16},{16,24},{24,0},{1,9},{9,17},{17,25},{25,1},{2,10},{10... | collective-permute-start | bytes 786440 | tf_op jit(solution)/shard_map/ppermute | solution.py:288
  81.8 4.2 %collective-permute-start.7 = (bf16[128,1024]{1,0:T(8,128)(2,1)S(1)}, bf16[128,1024]{1,0:T(8,128)(2,1)S(1)}, u32[]{:S(2)}, u32[]{:S(2)}) collective-permute-start(bf16[128,1024]{1,0:T(8,128)(2,1)S(1)} %slice.9), channel_id=1, source_target_pairs={{0,24},{8,0},{16,8},{24,16},{1,25},{9,1},{17,9},{25,17},{2,26},{10... | collective-permute-start | bytes 786440 | tf_op jit(solution)/shard_map/ppermute | solution.py:288
  86.1 3.2 %collective-permute-start.3 = (bf16[256,1024]{1,0:T(8,128)(2,1)S(1)}, bf16[256,1024]{1,0:T(8,128)(2,1)S(1)}, u32[]{:S(2)}, u32[]{:S(2)}) collective-permute-start(bf16[256,1024]{1,0:T(8,128)(2,1)S(1)} %collective-permute-done.2.refs_2_), channel_id=1, source_target_pairs={{0,1},{1,0},{2,3},{3,2},{4,5},{5,4},{6,7},{7,6},{8,9},{9,8},{10,11... | collective-permute-start | bytes 1572872 | tf_op jit(solution)/shard_map/ppermute | solution.py:290
  89.3 1.9 %collective-permute-start.5 = (bf16[256,1024]{1,0:T(8,128)(2,1)S(1)}, bf16[256,1024]{1,0:T(8,128)(2,1)S(1)}, u32[]{:S(2)}, u32[]{:S(2)}) collective-permute-start(bf16[256,1024]{1,0:T(8,128)(2,1)S(1)} %collective-permute-done.4.refs_4_), channel_id=1, source_target_pairs={{0,1},{1,0},{2,3},{3,2},{4,5},{5,4},{6,7},{7,6},{8,9},{9,8},{10,11... | collective-permute-start | bytes 1572872 | tf_op jit(solution)/shard_map/ppermute | solution.py:290
  91.3 3.2 %collective-permute-start.8 = (bf16[256,1024]{1,0:T(8,128)(2,1)S(1)}, bf16[256,1024]{1,0:T(8,128)(2,1)S(1)}, u32[]{:S(2)}, u32[]{:S(2)}) collective-permute-start(bf16[256,1024]{1,0:T(8,128)(2,1)S(1)} %constant_dynamic-update-slice_fusion.refs_6_), channel_id=1, source_target_pairs={{0,1},{1,0},{2,3},{3,2},{4,5},{5,4},{6,7},{7,6},{8,9},{9,8},{10,11... | collective-permute-start | bytes 1572872 | tf_op jit(solution)/shard_map/ppermute | solution.py:290
  94.5 1.9 %collective-permute-start.1 = (bf16[256,1024]{1,0:T(8,128)(2,1)S(1)}, bf16[256,1024]{1,0:T(8,128)(2,1)S(1)}, u32[]{:S(2)}, u32[]{:S(2)}) collective-permute-start(bf16[256,1024]{1,0:T(8,128)(2,1)S(1)} %all_gather.3.refs_0_), channel_id=1, source_target_pairs={{0,1},{1,0},{2,3},{3,2},{4,5},{5,4},{6,7},{7,6},{8,9},{9,8},{10,11... | collective-permute-start | bytes 1572872 | tf_op jit(solution)/shard_map/ppermute | solution.py:290
  97.2 6.3 %collective-permute-done.near_ref = bf16[8,32,2048]{2,1,0:T(8,128)(2,1)S(1)} collective-permute-done((bf16[8,32,2048]{2,1,0:T(8,128)(2,1)S(1)}, bf16[8,32,2048]{2,1,0:T(8,128)(2,1)S(1)}, u32[]{:S(2)}, u32[]{:S(2)}) %collective-permute-start) | collective-permute-done | bytes 1048608 | tf_op jit(solution)/shard_map/ppermute | solution.py:284
  103.6 3.1 %shard_map.64 = (bf16[512,1024]{1,0:T(8,128)(2,1)S(1)}, f32[16,2,128]{2,1,0:T(2,128)S(1)}) custom-call(bf16[512,2048]{1,0:T(8,128)(2,1)S(1)} %bitcast.4, f32[48,1024]{1,0:T(8,128)S(1)} %shard_map.63.levels_ref, bf16[256,1024]{1,0:T(8,128)(2,1)S(1)} %all_gather.3.refs_0_, bf16[256,1024]{1,0:T(8,128)(2,1)S(1)} %collective-permute-done.1.refs_1_, ...), custom_call_target="tpu_custom_call" | custom-call | tf_op jit(solution)/shard_map/pallas_call | solution.py:235
  106.7 1.0 copy-done.4
  107.7 11.1 %all_to_all.27.in_ref = f32[16,2,128]{2,1,0:T(2,128)S(1)} all-to-all(f32[16,2,128]{2,1,0:T(2,128)S(1)} %get-tuple-element.19), channel_id=1, replica_groups=mesh['y'=8,'zl'=2,'x'=4,'zh'=4,'k'=2] {'zl','zh','k'}, dimensions={0} | all-to-all | bytes 32768 | tf_op jit(solution)/shard_map/all_to_all | solution.py:302
  119.4 3.8 %all-to-all-start.4 = ((f32[32,2,128]{2,1,0:T(2,128)}), f32[32,2,128]{2,1,0:T(2,128)S(1)}, u32[]{:S(2)}, u32[]{:S(2)}) async-start(f32[32,2,128]{2,1,0:T(2,128)} %shard_map.66), calls=%async_computation.4 | async-start | bytes 65536 | tf_op jit(solution)/shard_map/all_to_all | solution.py:304
  123.3 3.4 %shard_map.65 = bf16[512,1024]{1,0:T(8,128)(2,1)} custom-call(bf16[512,1024]{1,0:T(8,128)(2,1)} %copy-done.4), custom_call_target="tpu_custom_call" | custom-call | flops 1073741824 | bytes 2097152 | tf_op jit(solution)/shard_map/pallas_call | solution.py:235
  126.6 5.4 %all-to-all-done.4.in_ref = f32[32,2,128]{2,1,0:T(2,128)S(1)} async-done(((f32[32,2,128]{2,1,0:T(2,128)}), f32[32,2,128]{2,1,0:T(2,128)S(1)}, u32[]{:S(2)}, u32[]{:S(2)}) %all-to-all-start.4) | async-done | bytes 32800 | tf_op jit(solution)/shard_map/all_to_all | solution.py:304
  132.0 0.8 shard_map.67
  (25 shorter events, 1.9 us)
Async XLA Ops:
  0.6 0.9 copy-start
  44.5 51.9 %copy-start.1 = (f32[1024]{0:T(1024)S(1)}, f32[1024]{0:T(1024)}, u32[]{:S(2)}) copy-start(f32[1024]{0:T(1024)} %param.6) | copy-start | bytes 12292
  44.5 52.0 %copy-start.2 = (f32[16]{0:T(128)S(1)}, f32[16]{0:T(128)}, u32[]{:S(2)}) copy-start(f32[16]{0:T(128)} %occ_ref.1) | copy-start | bytes 196
  44.5 52.0 %copy-start.3 = (s32[16]{0:T(128)S(1)}, s32[16]{0:T(128)}, u32[]{:S(2)}) copy-start(s32[16]{0:T(128)} %slot_ref.1) | copy-start | bytes 196
  44.5 32.8 %all-to-all-start.2 = ((bf16[8,32,2048]{2,1,0:T(8,128)(2,1)}), bf16[8,32,2048]{2,1,0:T(8,128)(2,1)S(1)}, u32[]{:S(2)}, u32[]{:S(2)}) async-start(bf16[8,32,2048]{2,1,0:T(8,128)(2,1)} %shard_map.60), calls=%async_computation.2 | async-start | bytes 2097152 | tf_op jit(solution)/shard_map/all_to_all | solution.py:281
  61.9 17.6 %collective-permute-start.2 = (bf16[256,1024]{1,0:T(8,128)(2,1)S(1)}, bf16[256,1024]{1,0:T(8,128)(2,1)S(1)}, u32[]{:S(2)}, u32[]{:S(2)}) collective-permute-start(bf16[256,1024]{1,0:T(8,128)(2,1)S(1)} %all_gather.3.refs_0_), channel_id=1, source_target_pairs={{0,8},{8,16},{16,24},{24,0},{1,9},{9,17},{17,25},{25,1},{2,10},{10... | collective-permute-start | bytes 1572872 | tf_op jit(solution)/shard_map/ppermute | solution.py:286
  64.3 17.5 %collective-permute-start.4 = (bf16[256,1024]{1,0:T(8,128)(2,1)S(1)}, bf16[256,1024]{1,0:T(8,128)(2,1)S(1)}, u32[]{:S(2)}, u32[]{:S(2)}) collective-permute-start(bf16[256,1024]{1,0:T(8,128)(2,1)S(1)} %all_gather.3.refs_0_), channel_id=1, source_target_pairs={{0,24},{8,0},{16,8},{24,16},{1,25},{9,1},{17,9},{25,17},{2,26},{10... | collective-permute-start | bytes 1572872 | tf_op jit(solution)/shard_map/ppermute | solution.py:286
  77.3 26.1 %collective-permute-start = (bf16[8,32,2048]{2,1,0:T(8,128)(2,1)S(1)}, bf16[8,32,2048]{2,1,0:T(8,128)(2,1)S(1)}, u32[]{:S(2)}, u32[]{:S(2)}) collective-permute-start(bf16[8,32,2048]{2,1,0:T(8,128)(2,1)S(1)} %all-to-all-done.2.own_ref), channel_id=1, source_target_pairs={{0,32},{32,0},{1,33},{33,1},{2,34},{34,2},{3,35},{35,3},{4,36},{36... | collective-permute-start | bytes 3145736 | tf_op jit(solution)/shard_map/ppermute | solution.py:284
  79.5 11.7 %collective-permute-start.6 = (bf16[128,1024]{1,0:T(8,128)(2,1)S(1)}, bf16[128,1024]{1,0:T(8,128)(2,1)S(1)}, u32[]{:S(2)}, u32[]{:S(2)}) collective-permute-start(bf16[128,1024]{1,0:T(8,128)(2,1)S(1)} %slice.8), channel_id=1, source_target_pairs={{0,8},{8,16},{16,24},{24,0},{1,9},{9,17},{17,25},{25,1},{2,10},{10... | collective-permute-start | bytes 786440 | tf_op jit(solution)/shard_map/ppermute | solution.py:288
  81.8 9.5 %collective-permute-start.7 = (bf16[128,1024]{1,0:T(8,128)(2,1)S(1)}, bf16[128,1024]{1,0:T(8,128)(2,1)S(1)}, u32[]{:S(2)}, u32[]{:S(2)}) collective-permute-start(bf16[128,1024]{1,0:T(8,128)(2,1)S(1)} %slice.9), channel_id=1, source_target_pairs={{0,24},{8,0},{16,8},{24,16},{1,25},{9,1},{17,9},{25,17},{2,26},{10... | collective-permute-start | bytes 786440 | tf_op jit(solution)/shard_map/ppermute | solution.py:288
  86.1 17.5 %collective-permute-start.3 = (bf16[256,1024]{1,0:T(8,128)(2,1)S(1)}, bf16[256,1024]{1,0:T(8,128)(2,1)S(1)}, u32[]{:S(2)}, u32[]{:S(2)}) collective-permute-start(bf16[256,1024]{1,0:T(8,128)(2,1)S(1)} %collective-permute-done.2.refs_2_), channel_id=1, source_target_pairs={{0,1},{1,0},{2,3},{3,2},{4,5},{5,4},{6,7},{7,6},{8,9},{9,8},{10,11... | collective-permute-start | bytes 1572872 | tf_op jit(solution)/shard_map/ppermute | solution.py:290
  89.3 14.3 %collective-permute-start.5 = (bf16[256,1024]{1,0:T(8,128)(2,1)S(1)}, bf16[256,1024]{1,0:T(8,128)(2,1)S(1)}, u32[]{:S(2)}, u32[]{:S(2)}) collective-permute-start(bf16[256,1024]{1,0:T(8,128)(2,1)S(1)} %collective-permute-done.4.refs_4_), channel_id=1, source_target_pairs={{0,1},{1,0},{2,3},{3,2},{4,5},{5,4},{6,7},{7,6},{8,9},{9,8},{10,11... | collective-permute-start | bytes 1572872 | tf_op jit(solution)/shard_map/ppermute | solution.py:290
  91.3 12.3 %collective-permute-start.8 = (bf16[256,1024]{1,0:T(8,128)(2,1)S(1)}, bf16[256,1024]{1,0:T(8,128)(2,1)S(1)}, u32[]{:S(2)}, u32[]{:S(2)}) collective-permute-start(bf16[256,1024]{1,0:T(8,128)(2,1)S(1)} %constant_dynamic-update-slice_fusion.refs_6_), channel_id=1, source_target_pairs={{0,1},{1,0},{2,3},{3,2},{4,5},{5,4},{6,7},{7,6},{8,9},{9,8},{10,11... | collective-permute-start | bytes 1572872 | tf_op jit(solution)/shard_map/ppermute | solution.py:290
  94.5 9.1 %collective-permute-start.1 = (bf16[256,1024]{1,0:T(8,128)(2,1)S(1)}, bf16[256,1024]{1,0:T(8,128)(2,1)S(1)}, u32[]{:S(2)}, u32[]{:S(2)}) collective-permute-start(bf16[256,1024]{1,0:T(8,128)(2,1)S(1)} %all_gather.3.refs_0_), channel_id=1, source_target_pairs={{0,1},{1,0},{2,3},{3,2},{4,5},{5,4},{6,7},{7,6},{8,9},{9,8},{10,11... | collective-permute-start | bytes 1572872 | tf_op jit(solution)/shard_map/ppermute | solution.py:290
  106.7 1.0 copy-start.4
  119.4 12.6 %all-to-all-start.4 = ((f32[32,2,128]{2,1,0:T(2,128)}), f32[32,2,128]{2,1,0:T(2,128)S(1)}, u32[]{:S(2)}, u32[]{:S(2)}) async-start(f32[32,2,128]{2,1,0:T(2,128)} %shard_map.66), calls=%async_computation.4 | async-start | bytes 65536 | tf_op jit(solution)/shard_map/all_to_all | solution.py:304

commit v6 on v5

--- a/solution.py
+++ b/solution.py
@@ -52,7 +52,7 @@
         a2_ref[2 * t + 1] = odd
 
 
-def first_kernel(in_ref, out_ref):
+def first_kernel(in_ref, out_ref, one_ref, sems):
     own_k, own_x = lax.axis_index("k"), lax.axis_index("x")
     for n, (d, rel) in enumerate(ARRIVAL):
         k = (own_k + rel) % K
@@ -61,9 +61,13 @@
             base = (x * ZH + 2 * m) * K + k
             top, bottom = pair_halves(in_ref[base], in_ref[base + K])
             lanes = (n * ZH + 2 * m) * PB
-            for y in range(Y):
-                out_ref[y, 0 : WA // 2, lanes : lanes + 128] = top
-                out_ref[y, WA // 2 : WA, lanes : lanes + 128] = bottom
+            one_ref[0 : WA // 2, lanes : lanes + 128] = top
+            one_ref[WA // 2 : WA, lanes : lanes + 128] = bottom
+    copies = [pltpu.make_async_copy(one_ref, out_ref.at[y], sems.at[y]) for y in range(Y)]
+    for copy in copies:
+        copy.start()
+    for copy in copies:
+        copy.wait()
 
 
 def place_kernel(own_ref, near_ref, out_ref):
@@ -274,7 +278,13 @@
         [factors.reshape(PB, NV)],
     )
     b1 = lax.all_to_all(a1, ("x", "zh", "k"), 0, 0, tiled=True)
-    first = call(first_kernel, shape((Y, WA, AUX)), [b1])
+    first = call(
+        first_kernel,
+        shape((Y, WA, AUX)),
+        [b1],
+        scratch=[pltpu.VMEM((WA, AUX), jnp.bfloat16), pltpu.SemaphoreType.DMA((Y,))],
+        out=ANY,
+    )
     a2, _ = lax.optimization_barrier((a2, first))
     b2 = lax.all_to_all(a2, ("y", "zl"), 0, 0, tiled=True)
     first, b2 = lax.optimization_barrier((first, b2))
@@ -300,6 +310,7 @@
     ratio, energy = run_main(left, levels, blocks)
     amp = run_order(ratio)
     energy = lax.all_to_all(energy, ("zl", "zh", "k"), 0, 0, tiled=True)
+    energy, amp = lax.optimization_barrier((energy, amp))
     energy = call(middle_kernel, shape((Y * X, 2, 128), f32), [energy])
     energy = lax.all_to_all(energy, ("y", "x"), 0, 0, tiled=True)
     return amp.reshape(NOCC, WA, COLS), call(last_kernel, shape((NOCC, NOCC), f32), [energy])

time: 133 us -> 133 us (level)
  waiting for transfers between devices: 20.6 us -> 19.2 us
    all_to_all x1, waiting for transfers between devices: 5.37 us -> 4 us  [per_device(): energy = lax.all_to_all(energy, ('zl', 'zh', 'k'), 0, 0, tiled=True)]
where the time goes in v6:
time: 133 us
  blocking collectives  66.8 us (50%)
  starting transfers between devices  33.7 us (25%)
  waiting for transfers between devices  19.2 us (14%)
  Pallas kernels  10.1 us (8%)
  local copies, waits for them, and re-layouts  1.96 us (1%)
    all_to_all x1, blocking collectives, per_device(): b1 = lax.all_to_all(a1, ('x', 'zh', 'k'), 0, 0, tiled=True)  25.6 us
    all_to_all x1, blocking collectives, per_device(): b2 = lax.all_to_all(a2, ('y', 'zl'), 0, 0, tiled=True)  16 us
    all_gather x1, blocking collectives, per_device(): second = lax.all_gather(second, 'zh', axis=0, tiled=True)  13.6 us
    all_to_all x1, blocking collectives, per_device(): energy = lax.all_to_all(energy, ('y', 'x'), 0, 0, tiled=True)  11.7 us
    ppermute x4, starting transfers between devices, per_device(): other = [lax.ppermute(block, 'k', [(0, 1), (1, 0)]) for block in mine]  10.3 us
    pallas_call x9, Pallas kernels, call(): pl.pallas_call(kernel, out_shape=out_shape, in_specs=kinds, out_specs=jax...  10.1 us
    all_to_all x1, waiting for transfers between devices, per_device(): own = lax.all_to_all(first, 'y', 0, 0, tiled=True)  8.94 us
    ppermute x1, waiting for transfers between devices, per_device(): near = lax.ppermute(own, 'zl', [(0, 1), (1, 0)])  6.28 us
  transfers between devices with their start and end apart: 11, of which 3 were waited for; matrix products, arithmetic and copies ran while one was open for 0% of the time, Pallas kernels for 3%

profile of v6, /device:TPU:1, one launch (start us, length us, event | category | flops | bytes accessed | tf_op | source)
XLA Modules:
  0.0 132.7 jit_solution(9163015348781784968)
XLA Ops:
  0.6 0.9 copy-done
  1.7 25.6 %all_to_all.25.in_ref = bf16[32,16,128]{2,1,0:T(8,128)(2,1)S(1)} all-to-all(bf16[32,16,128]{2,1,0:T(8,128)(2,1)S(1)} %get-tuple-element.13), channel_id=1, replica_groups=mesh['y'=8,'zl'=2,'x'=4,'zh'=4,'k'=2] {'x','zh','k'}, dimensions={0} | all-to-all | bytes 262144 | tf_op jit(solution)/shard_map/all_to_all | solution.py:280
  27.3 1.1 shard_map.60
  28.4 16.0 %all_to_all.26.in_ref = bf16[16,32,128]{2,1,0:T(8,128)(2,1)S(1)} all-to-all(bf16[16,32,128]{2,1,0:T(8,128)(2,1)S(1)} %get-tuple-element.15), channel_id=1, replica_groups=mesh['y'=8,'zl'=2,'x'=4,'zh'=4,'k'=2] {'y','zl'}, dimensions={0} | all-to-all | bytes 262144 | tf_op jit(solution)/shard_map/all_to_all | solution.py:289
  44.4 3.7 %all-to-all-start.2 = ((bf16[8,32,2048]{2,1,0:T(8,128)(2,1)}), bf16[8,32,2048]{2,1,0:T(8,128)(2,1)S(1)}, u32[]{:S(2)}, u32[]{:S(2)}) async-start(bf16[8,32,2048]{2,1,0:T(8,128)(2,1)} %shard_map.60), calls=%async_computation.2 | async-start | bytes 2097152 | tf_op jit(solution)/shard_map/all_to_all | solution.py:291
  48.2 13.6 %all_gather.3.refs_0_ = bf16[256,1024]{1,0:T(8,128)(2,1)S(1)} all-gather(bf16[64,1024]{1,0:T(8,128)(2,1)S(1)} %shard_map.61), channel_id=1, replica_groups=mesh['y'=8,'zl'=2,'x'=4,'zh'=4,'k'=2] {'zh'}, dimensions={0}, use_global_device_ids=true | all-gather | bytes 655360 | tf_op jit(solution)/shard_map/all_gather | solution.py:293
  61.8 2.5 %collective-permute-start.2 = (bf16[256,1024]{1,0:T(8,128)(2,1)S(1)}, bf16[256,1024]{1,0:T(8,128)(2,1)S(1)}, u32[]{:S(2)}, u32[]{:S(2)}) collective-permute-start(bf16[256,1024]{1,0:T(8,128)(2,1)S(1)} %all_gather.3.refs_0_), channel_id=1, source_target_pairs={{0,8},{8,16},{16,24},{24,0},{1,9},{9,17},{17,25},{25,1},{2,10},{10... | collective-permute-start | bytes 1572872 | tf_op jit(solution)/shard_map/ppermute | solution.py:296
  64.2 4.0 %collective-permute-start.4 = (bf16[256,1024]{1,0:T(8,128)(2,1)S(1)}, bf16[256,1024]{1,0:T(8,128)(2,1)S(1)}, u32[]{:S(2)}, u32[]{:S(2)}) collective-permute-start(bf16[256,1024]{1,0:T(8,128)(2,1)S(1)} %all_gather.3.refs_0_), channel_id=1, source_target_pairs={{0,24},{8,0},{16,8},{24,16},{1,25},{9,1},{17,9},{25,17},{2,26},{10... | collective-permute-start | bytes 1572872 | tf_op jit(solution)/shard_map/ppermute | solution.py:296
  68.3 8.9 %all-to-all-done.2.own_ref = bf16[8,32,2048]{2,1,0:T(8,128)(2,1)S(1)} async-done(((bf16[8,32,2048]{2,1,0:T(8,128)(2,1)}), bf16[8,32,2048]{2,1,0:T(8,128)(2,1)S(1)}, u32[]{:S(2)}, u32[]{:S(2)}) %all-to-all-start.2) | async-done | bytes 1048608 | tf_op jit(solution)/shard_map/all_to_all | solution.py:291
  77.2 2.2 %collective-permute-start = (bf16[8,32,2048]{2,1,0:T(8,128)(2,1)S(1)}, bf16[8,32,2048]{2,1,0:T(8,128)(2,1)S(1)}, u32[]{:S(2)}, u32[]{:S(2)}) collective-permute-start(bf16[8,32,2048]{2,1,0:T(8,128)(2,1)S(1)} %all-to-all-done.2.own_ref), channel_id=1, source_target_pairs={{0,32},{32,0},{1,33},{33,1},{2,34},{34,2},{3,35},{35,3},{4,36},{36... | collective-permute-start | bytes 3145736 | tf_op jit(solution)/shard_map/ppermute | solution.py:294
  79.4 2.3 %collective-permute-start.6 = (bf16[128,1024]{1,0:T(8,128)(2,1)S(1)}, bf16[128,1024]{1,0:T(8,128)(2,1)S(1)}, u32[]{:S(2)}, u32[]{:S(2)}) collective-permute-start(bf16[128,1024]{1,0:T(8,128)(2,1)S(1)} %slice.8), channel_id=1, source_target_pairs={{0,8},{8,16},{16,24},{24,0},{1,9},{9,17},{17,25},{25,1},{2,10},{10... | collective-permute-start | bytes 786440 | tf_op jit(solution)/shard_map/ppermute | solution.py:298
  81.7 4.2 %collective-permute-start.7 = (bf16[128,1024]{1,0:T(8,128)(2,1)S(1)}, bf16[128,1024]{1,0:T(8,128)(2,1)S(1)}, u32[]{:S(2)}, u32[]{:S(2)}) collective-permute-start(bf16[128,1024]{1,0:T(8,128)(2,1)S(1)} %slice.9), channel_id=1, source_target_pairs={{0,24},{8,0},{16,8},{24,16},{1,25},{9,1},{17,9},{25,17},{2,26},{10... | collective-permute-start | bytes 786440 | tf_op jit(solution)/shard_map/ppermute | solution.py:298
  86.0 3.2 %collective-permute-start.3 = (bf16[256,1024]{1,0:T(8,128)(2,1)S(1)}, bf16[256,1024]{1,0:T(8,128)(2,1)S(1)}, u32[]{:S(2)}, u32[]{:S(2)}) collective-permute-start(bf16[256,1024]{1,0:T(8,128)(2,1)S(1)} %collective-permute-done.2.refs_2_), channel_id=1, source_target_pairs={{0,1},{1,0},{2,3},{3,2},{4,5},{5,4},{6,7},{7,6},{8,9},{9,8},{10,11... | collective-permute-start | bytes 1572872 | tf_op jit(solution)/shard_map/ppermute | solution.py:300
  89.2 1.9 %collective-permute-start.5 = (bf16[256,1024]{1,0:T(8,128)(2,1)S(1)}, bf16[256,1024]{1,0:T(8,128)(2,1)S(1)}, u32[]{:S(2)}, u32[]{:S(2)}) collective-permute-start(bf16[256,1024]{1,0:T(8,128)(2,1)S(1)} %collective-permute-done.4.refs_4_), channel_id=1, source_target_pairs={{0,1},{1,0},{2,3},{3,2},{4,5},{5,4},{6,7},{7,6},{8,9},{9,8},{10,11... | collective-permute-start | bytes 1572872 | tf_op jit(solution)/shard_map/ppermute | solution.py:300
  91.2 3.2 %collective-permute-start.8 = (bf16[256,1024]{1,0:T(8,128)(2,1)S(1)}, bf16[256,1024]{1,0:T(8,128)(2,1)S(1)}, u32[]{:S(2)}, u32[]{:S(2)}) collective-permute-start(bf16[256,1024]{1,0:T(8,128)(2,1)S(1)} %constant_dynamic-update-slice_fusion.refs_6_), channel_id=1, source_target_pairs={{0,1},{1,0},{2,3},{3,2},{4,5},{5,4},{6,7},{7,6},{8,9},{9,8},{10,11... | collective-permute-start | bytes 1572872 | tf_op jit(solution)/shard_map/ppermute | solution.py:300
  94.4 1.9 %collective-permute-start.1 = (bf16[256,1024]{1,0:T(8,128)(2,1)S(1)}, bf16[256,1024]{1,0:T(8,128)(2,1)S(1)}, u32[]{:S(2)}, u32[]{:S(2)}) collective-permute-start(bf16[256,1024]{1,0:T(8,128)(2,1)S(1)} %all_gather.3.refs_0_), channel_id=1, source_target_pairs={{0,1},{1,0},{2,3},{3,2},{4,5},{5,4},{6,7},{7,6},{8,9},{9,8},{10,11... | collective-permute-start | bytes 1572872 | tf_op jit(solution)/shard_map/ppermute | solution.py:300
  97.0 6.3 %collective-permute-done.near_ref = bf16[8,32,2048]{2,1,0:T(8,128)(2,1)S(1)} collective-permute-done((bf16[8,32,2048]{2,1,0:T(8,128)(2,1)S(1)}, bf16[8,32,2048]{2,1,0:T(8,128)(2,1)S(1)}, u32[]{:S(2)}, u32[]{:S(2)}) %collective-permute-start) | collective-permute-done | bytes 1048608 | tf_op jit(solution)/shard_map/ppermute | solution.py:294
  103.5 3.7 %shard_map.64 = (bf16[512,1024]{1,0:T(8,128)(2,1)S(1)}, f32[16,2,128]{2,1,0:T(2,128)}) custom-call(bf16[512,2048]{1,0:T(8,128)(2,1)S(1)} %bitcast.4, f32[48,1024]{1,0:T(8,128)S(1)} %shard_map.63.levels_ref, bf16[256,1024]{1,0:T(8,128)(2,1)S(1)} %all_gather.3.refs_0_, bf16[256,1024]{1,0:T(8,128)(2,1)S(1)} %collective-permute-done.1.refs_1_, ...), custom_call_target="tpu_custom_call" | custom-call | tf_op jit(solution)/shard_map/pallas_call | solution.py:239
  107.2 1.0 copy-done.4
  108.2 4.6 %all-to-all-start.3 = ((f32[16,2,128]{2,1,0:T(2,128)}), f32[16,2,128]{2,1,0:T(2,128)S(1)}, u32[]{:S(2)}, u32[]{:S(2)}) async-start(f32[16,2,128]{2,1,0:T(2,128)} %get-tuple-element.20), calls=%async_computation.3 | async-start | bytes 32768 | tf_op jit(solution)/shard_map/all_to_all | solution.py:312
  112.8 3.3 %shard_map.65 = bf16[512,1024]{1,0:T(8,128)(2,1)} custom-call(bf16[512,1024]{1,0:T(8,128)(2,1)} %copy-done.4), custom_call_target="tpu_custom_call" | custom-call | flops 1073741824 | bytes 2097152 | tf_op jit(solution)/shard_map/pallas_call | solution.py:239
  116.2 4.0 %all-to-all-done.3.in_ref = f32[16,2,128]{2,1,0:T(2,128)S(1)} async-done(((f32[16,2,128]{2,1,0:T(2,128)}), f32[16,2,128]{2,1,0:T(2,128)S(1)}, u32[]{:S(2)}, u32[]{:S(2)}) %all-to-all-start.3) | async-done | bytes 16416 | tf_op jit(solution)/shard_map/all_to_all | solution.py:312
  120.2 11.7 %all_to_all.27.in_ref = f32[32,2,128]{2,1,0:T(2,128)S(1)} all-to-all(f32[32,2,128]{2,1,0:T(2,128)S(1)} %shard_map.66), channel_id=1, replica_groups=mesh['y'=8,'zl'=2,'x'=4,'zh'=4,'k'=2] {'y','x'}, dimensions={0} | all-to-all | bytes 65536 | tf_op jit(solution)/shard_map/all_to_all | solution.py:315
  131.9 0.8 shard_map.67
  (25 shorter events, 1.3 us)
Async XLA Ops:
  0.6 0.9 copy-start
  44.4 51.9 %copy-start.1 = (f32[1024]{0:T(1024)S(1)}, f32[1024]{0:T(1024)}, u32[]{:S(2)}) copy-start(f32[1024]{0:T(1024)} %param.6) | copy-start | bytes 12292
  44.4 52.0 %copy-start.2 = (f32[16]{0:T(128)S(1)}, f32[16]{0:T(128)}, u32[]{:S(2)}) copy-start(f32[16]{0:T(128)} %occ_ref.1) | copy-start | bytes 196
  44.4 52.0 %copy-start.3 = (s32[16]{0:T(128)S(1)}, s32[16]{0:T(128)}, u32[]{:S(2)}) copy-start(s32[16]{0:T(128)} %slot_ref.1) | copy-start | bytes 196
  44.4 32.8 %all-to-all-start.2 = ((bf16[8,32,2048]{2,1,0:T(8,128)(2,1)}), bf16[8,32,2048]{2,1,0:T(8,128)(2,1)S(1)}, u32[]{:S(2)}, u32[]{:S(2)}) async-start(bf16[8,32,2048]{2,1,0:T(8,128)(2,1)} %shard_map.60), calls=%async_computation.2 | async-start | bytes 2097152 | tf_op jit(solution)/shard_map/all_to_all | solution.py:291
  61.8 17.6 %collective-permute-start.2 = (bf16[256,1024]{1,0:T(8,128)(2,1)S(1)}, bf16[256,1024]{1,0:T(8,128)(2,1)S(1)}, u32[]{:S(2)}, u32[]{:S(2)}) collective-permute-start(bf16[256,1024]{1,0:T(8,128)(2,1)S(1)} %all_gather.3.refs_0_), channel_id=1, source_target_pairs={{0,8},{8,16},{16,24},{24,0},{1,9},{9,17},{17,25},{25,1},{2,10},{10... | collective-permute-start | bytes 1572872 | tf_op jit(solution)/shard_map/ppermute | solution.py:296
  64.2 17.5 %collective-permute-start.4 = (bf16[256,1024]{1,0:T(8,128)(2,1)S(1)}, bf16[256,1024]{1,0:T(8,128)(2,1)S(1)}, u32[]{:S(2)}, u32[]{:S(2)}) collective-permute-start(bf16[256,1024]{1,0:T(8,128)(2,1)S(1)} %all_gather.3.refs_0_), channel_id=1, source_target_pairs={{0,24},{8,0},{16,8},{24,16},{1,25},{9,1},{17,9},{25,17},{2,26},{10... | collective-permute-start | bytes 1572872 | tf_op jit(solution)/shard_map/ppermute | solution.py:296
  77.2 26.1 %collective-permute-start = (bf16[8,32,2048]{2,1,0:T(8,128)(2,1)S(1)}, bf16[8,32,2048]{2,1,0:T(8,128)(2,1)S(1)}, u32[]{:S(2)}, u32[]{:S(2)}) collective-permute-start(bf16[8,32,2048]{2,1,0:T(8,128)(2,1)S(1)} %all-to-all-done.2.own_ref), channel_id=1, source_target_pairs={{0,32},{32,0},{1,33},{33,1},{2,34},{34,2},{3,35},{35,3},{4,36},{36... | collective-permute-start | bytes 3145736 | tf_op jit(solution)/shard_map/ppermute | solution.py:294
  79.4 11.7 %collective-permute-start.6 = (bf16[128,1024]{1,0:T(8,128)(2,1)S(1)}, bf16[128,1024]{1,0:T(8,128)(2,1)S(1)}, u32[]{:S(2)}, u32[]{:S(2)}) collective-permute-start(bf16[128,1024]{1,0:T(8,128)(2,1)S(1)} %slice.8), channel_id=1, source_target_pairs={{0,8},{8,16},{16,24},{24,0},{1,9},{9,17},{17,25},{25,1},{2,10},{10... | collective-permute-start | bytes 786440 | tf_op jit(solution)/shard_map/ppermute | solution.py:298
  81.7 9.5 %collective-permute-start.7 = (bf16[128,1024]{1,0:T(8,128)(2,1)S(1)}, bf16[128,1024]{1,0:T(8,128)(2,1)S(1)}, u32[]{:S(2)}, u32[]{:S(2)}) collective-permute-start(bf16[128,1024]{1,0:T(8,128)(2,1)S(1)} %slice.9), channel_id=1, source_target_pairs={{0,24},{8,0},{16,8},{24,16},{1,25},{9,1},{17,9},{25,17},{2,26},{10... | collective-permute-start | bytes 786440 | tf_op jit(solution)/shard_map/ppermute | solution.py:298
  86.0 17.5 %collective-permute-start.3 = (bf16[256,1024]{1,0:T(8,128)(2,1)S(1)}, bf16[256,1024]{1,0:T(8,128)(2,1)S(1)}, u32[]{:S(2)}, u32[]{:S(2)}) collective-permute-start(bf16[256,1024]{1,0:T(8,128)(2,1)S(1)} %collective-permute-done.2.refs_2_), channel_id=1, source_target_pairs={{0,1},{1,0},{2,3},{3,2},{4,5},{5,4},{6,7},{7,6},{8,9},{9,8},{10,11... | collective-permute-start | bytes 1572872 | tf_op jit(solution)/shard_map/ppermute | solution.py:300
  89.2 14.3 %collective-permute-start.5 = (bf16[256,1024]{1,0:T(8,128)(2,1)S(1)}, bf16[256,1024]{1,0:T(8,128)(2,1)S(1)}, u32[]{:S(2)}, u32[]{:S(2)}) collective-permute-start(bf16[256,1024]{1,0:T(8,128)(2,1)S(1)} %collective-permute-done.4.refs_4_), channel_id=1, source_target_pairs={{0,1},{1,0},{2,3},{3,2},{4,5},{5,4},{6,7},{7,6},{8,9},{9,8},{10,11... | collective-permute-start | bytes 1572872 | tf_op jit(solution)/shard_map/ppermute | solution.py:300
  91.2 12.3 %collective-permute-start.8 = (bf16[256,1024]{1,0:T(8,128)(2,1)S(1)}, bf16[256,1024]{1,0:T(8,128)(2,1)S(1)}, u32[]{:S(2)}, u32[]{:S(2)}) collective-permute-start(bf16[256,1024]{1,0:T(8,128)(2,1)S(1)} %constant_dynamic-update-slice_fusion.refs_6_), channel_id=1, source_target_pairs={{0,1},{1,0},{2,3},{3,2},{4,5},{5,4},{6,7},{7,6},{8,9},{9,8},{10,11... | collective-permute-start | bytes 1572872 | tf_op jit(solution)/shard_map/ppermute | solution.py:300
  94.4 9.1 %collective-permute-start.1 = (bf16[256,1024]{1,0:T(8,128)(2,1)S(1)}, bf16[256,1024]{1,0:T(8,128)(2,1)S(1)}, u32[]{:S(2)}, u32[]{:S(2)}) collective-permute-start(bf16[256,1024]{1,0:T(8,128)(2,1)S(1)} %all_gather.3.refs_0_), channel_id=1, source_target_pairs={{0,1},{1,0},{2,3},{3,2},{4,5},{5,4},{6,7},{7,6},{8,9},{9,8},{10,11... | collective-permute-start | bytes 1572872 | tf_op jit(solution)/shard_map/ppermute | solution.py:300
  107.2 1.0 copy-start.4
  108.2 12.0 %all-to-all-start.3 = ((f32[16,2,128]{2,1,0:T(2,128)}), f32[16,2,128]{2,1,0:T(2,128)S(1)}, u32[]{:S(2)}, u32[]{:S(2)}) async-start(f32[16,2,128]{2,1,0:T(2,128)} %get-tuple-element.20), calls=%async_computation.3 | async-start | bytes 32768 | tf_op jit(solution)/shard_map/all_to_all | solution.py:312

commit v7 on v6

--- a/solution.py
+++ b/solution.py
@@ -70,10 +70,15 @@
         copy.wait()
 
 
-def place_kernel(own_ref, near_ref, out_ref):
+def own_kernel(own_ref, out_ref):
     zl = lax.axis_index("zl")
     for y in range(Y):
         out_ref[y, zl] = own_ref[y]
+
+
+def near_kernel(held_ref, near_ref, out_ref):
+    zl = lax.axis_index("zl")
+    for y in range(Y):
         out_ref[y, 1 - zl] = near_ref[y]
 
 
@@ -233,7 +238,7 @@
     return jax.ShapeDtypeStruct(dims, dtype)
 
 
-def call(kernel, out_shape, operands, in_specs=None, scratch=(), flops=0, out=VMEM, limit=16):
+def call(kernel, out_shape, operands, in_specs=None, scratch=(), flops=0, out=VMEM, limit=16, aliases=None):
     kinds = in_specs or [VMEM] * len(operands)
     cost = pl.CostEstimate(flops=flops, bytes_accessed=4 * ROWS * COLS, transcendentals=0) if flops else None
     return pl.pallas_call(
@@ -242,6 +247,7 @@
         in_specs=kinds,
         out_specs=jax.tree.map(lambda _: out, out_shape),
         scratch_shapes=scratch,
+        input_output_aliases=aliases or {},
         compiler_params=pltpu.CompilerParams(vmem_limit_bytes=limit * 1024 * 1024),
         cost_estimate=cost,
     )(*operands)
@@ -299,7 +305,8 @@
     mine = [second, below, above, jnp.concatenate(far, axis=0)]
     other = [lax.ppermute(block, "k", [(0, 1), (1, 0)]) for block in mine]
     blocks = [side[n] for n in range(4) for side in (mine, other)]
-    left = call(place_kernel, shape((Y, ZL, WA, AUX)), [own, near]).reshape(ROWS, AUX)
+    held = call(own_kernel, shape((Y, ZL, WA, AUX)), [own])
+    left = call(near_kernel, shape((Y, ZL, WA, AUX)), [held, near], aliases={0: 0}).reshape(ROWS, AUX)
     levels = call(
         levels_kernel,
         shape((WA + NOCC, COLS), f32),

time: 133 us -> 133 us (level)
    pallas_call x9 -> x10, Pallas kernels: 10.1 us -> 10.2 us  [call(): pl.pallas_call(kernel, out_shape=out_shape, in_specs=kinds, out_specs=jax...]
where the time goes in v7:
time: 133 us
  blocking collectives  66.8 us (50%)
  starting transfers between devices  33.7 us (25%)
  waiting for transfers between devices  19.1 us (14%)
  Pallas kernels  10.2 us (8%)
  local copies, waits for them, and re-layouts  1.96 us (1%)
    all_to_all x1, blocking collectives, per_device(): b1 = lax.all_to_all(a1, ('x', 'zh', 'k'), 0, 0, tiled=True)  25.6 us
    all_to_all x1, blocking collectives, per_device(): b2 = lax.all_to_all(a2, ('y', 'zl'), 0, 0, tiled=True)  16 us
    all_gather x1, blocking collectives, per_device(): second = lax.all_gather(second, 'zh', axis=0, tiled=True)  13.6 us
    all_to_all x1, blocking collectives, per_device(): energy = lax.all_to_all(energy, ('y', 'x'), 0, 0, tiled=True)  11.7 us
    ppermute x4, starting transfers between devices, per_device(): other = [lax.ppermute(block, 'k', [(0, 1), (1, 0)]) for block in mine]  10.3 us
    pallas_call x10, Pallas kernels, call(): pl.pallas_call(kernel, out_shape=out_shape, in_specs=kinds, out_specs=jax...  10.2 us
    all_to_all x1, waiting for transfers between devices, per_device(): own = lax.all_to_all(first, 'y', 0, 0, tiled=True)  8.94 us
    ppermute x1, waiting for transfers between devices, per_device(): near = lax.ppermute(own, 'zl', [(0, 1), (1, 0)])  6.19 us
  transfers between devices with their start and end apart: 11, of which 3 were waited for; matrix products, arithmetic and copies ran while one was open for 0% of the time, Pallas kernels for 3%

profile of v7, /device:TPU:1, one launch (start us, length us, event | category | flops | bytes accessed | tf_op | source)
XLA Modules:
  0.0 132.7 jit_solution(10247878875626155971)
XLA Ops:
  0.6 0.9 copy-done
  1.7 25.6 %all_to_all.25.in_ref = bf16[32,16,128]{2,1,0:T(8,128)(2,1)S(1)} all-to-all(bf16[32,16,128]{2,1,0:T(8,128)(2,1)S(1)} %get-tuple-element.13), channel_id=1, replica_groups=mesh['y'=8,'zl'=2,'x'=4,'zh'=4,'k'=2] {'x','zh','k'}, dimensions={0} | all-to-all | bytes 262144 | tf_op jit(solution)/shard_map/all_to_all | solution.py:286
  27.3 1.1 shard_map.60
  28.4 16.0 %all_to_all.26.in_ref = bf16[16,32,128]{2,1,0:T(8,128)(2,1)S(1)} all-to-all(bf16[16,32,128]{2,1,0:T(8,128)(2,1)S(1)} %get-tuple-element.15), channel_id=1, replica_groups=mesh['y'=8,'zl'=2,'x'=4,'zh'=4,'k'=2] {'y','zl'}, dimensions={0} | all-to-all | bytes 262144 | tf_op jit(solution)/shard_map/all_to_all | solution.py:295
  44.4 3.7 %all-to-all-start.2 = ((bf16[8,32,2048]{2,1,0:T(8,128)(2,1)}), bf16[8,32,2048]{2,1,0:T(8,128)(2,1)S(1)}, u32[]{:S(2)}, u32[]{:S(2)}) async-start(bf16[8,32,2048]{2,1,0:T(8,128)(2,1)} %shard_map.60), calls=%async_computation.2 | async-start | bytes 2097152 | tf_op jit(solution)/shard_map/all_to_all | solution.py:297
  48.2 13.6 %all_gather.3.refs_0_ = bf16[256,1024]{1,0:T(8,128)(2,1)S(1)} all-gather(bf16[64,1024]{1,0:T(8,128)(2,1)S(1)} %shard_map.61), channel_id=1, replica_groups=mesh['y'=8,'zl'=2,'x'=4,'zh'=4,'k'=2] {'zh'}, dimensions={0}, use_global_device_ids=true | all-gather | bytes 655360 | tf_op jit(solution)/shard_map/all_gather | solution.py:299
  61.8 2.5 %collective-permute-start.2 = (bf16[256,1024]{1,0:T(8,128)(2,1)S(1)}, bf16[256,1024]{1,0:T(8,128)(2,1)S(1)}, u32[]{:S(2)}, u32[]{:S(2)}) collective-permute-start(bf16[256,1024]{1,0:T(8,128)(2,1)S(1)} %all_gather.3.refs_0_), channel_id=1, source_target_pairs={{0,8},{8,16},{16,24},{24,0},{1,9},{9,17},{17,25},{25,1},{2,10},{10... | collective-permute-start | bytes 1572872 | tf_op jit(solution)/shard_map/ppermute | solution.py:302
  64.2 4.0 %collective-permute-start.4 = (bf16[256,1024]{1,0:T(8,128)(2,1)S(1)}, bf16[256,1024]{1,0:T(8,128)(2,1)S(1)}, u32[]{:S(2)}, u32[]{:S(2)}) collective-permute-start(bf16[256,1024]{1,0:T(8,128)(2,1)S(1)} %all_gather.3.refs_0_), channel_id=1, source_target_pairs={{0,24},{8,0},{16,8},{24,16},{1,25},{9,1},{17,9},{25,17},{2,26},{10... | collective-permute-start | bytes 1572872 | tf_op jit(solution)/shard_map/ppermute | solution.py:302
  68.3 8.9 %all-to-all-done.2.own_ref = bf16[8,32,2048]{2,1,0:T(8,128)(2,1)S(1)} async-done(((bf16[8,32,2048]{2,1,0:T(8,128)(2,1)}), bf16[8,32,2048]{2,1,0:T(8,128)(2,1)S(1)}, u32[]{:S(2)}, u32[]{:S(2)}) %all-to-all-start.2) | async-done | bytes 1048608 | tf_op jit(solution)/shard_map/all_to_all | solution.py:297
  77.2 2.2 %collective-permute-start = (bf16[8,32,2048]{2,1,0:T(8,128)(2,1)S(1)}, bf16[8,32,2048]{2,1,0:T(8,128)(2,1)S(1)}, u32[]{:S(2)}, u32[]{:S(2)}) collective-permute-start(bf16[8,32,2048]{2,1,0:T(8,128)(2,1)S(1)} %all-to-all-done.2.own_ref), channel_id=1, source_target_pairs={{0,32},{32,0},{1,33},{33,1},{2,34},{34,2},{3,35},{35,3},{4,36},{36... | collective-permute-start | bytes 3145736 | tf_op jit(solution)/shard_map/ppermute | solution.py:300
  79.4 2.3 %collective-permute-start.6 = (bf16[128,1024]{1,0:T(8,128)(2,1)S(1)}, bf16[128,1024]{1,0:T(8,128)(2,1)S(1)}, u32[]{:S(2)}, u32[]{:S(2)}) collective-permute-start(bf16[128,1024]{1,0:T(8,128)(2,1)S(1)} %slice.8), channel_id=1, source_target_pairs={{0,8},{8,16},{16,24},{24,0},{1,9},{9,17},{17,25},{25,1},{2,10},{10... | collective-permute-start | bytes 786440 | tf_op jit(solution)/shard_map/ppermute | solution.py:304
  81.7 4.2 %collective-permute-start.7 = (bf16[128,1024]{1,0:T(8,128)(2,1)S(1)}, bf16[128,1024]{1,0:T(8,128)(2,1)S(1)}, u32[]{:S(2)}, u32[]{:S(2)}) collective-permute-start(bf16[128,1024]{1,0:T(8,128)(2,1)S(1)} %slice.9), channel_id=1, source_target_pairs={{0,24},{8,0},{16,8},{24,16},{1,25},{9,1},{17,9},{25,17},{2,26},{10... | collective-permute-start | bytes 786440 | tf_op jit(solution)/shard_map/ppermute | solution.py:304
  86.0 3.2 %collective-permute-start.3 = (bf16[256,1024]{1,0:T(8,128)(2,1)S(1)}, bf16[256,1024]{1,0:T(8,128)(2,1)S(1)}, u32[]{:S(2)}, u32[]{:S(2)}) collective-permute-start(bf16[256,1024]{1,0:T(8,128)(2,1)S(1)} %collective-permute-done.2.refs_2_), channel_id=1, source_target_pairs={{0,1},{1,0},{2,3},{3,2},{4,5},{5,4},{6,7},{7,6},{8,9},{9,8},{10,11... | collective-permute-start | bytes 1572872 | tf_op jit(solution)/shard_map/ppermute | solution.py:306
  89.2 1.9 %collective-permute-start.5 = (bf16[256,1024]{1,0:T(8,128)(2,1)S(1)}, bf16[256,1024]{1,0:T(8,128)(2,1)S(1)}, u32[]{:S(2)}, u32[]{:S(2)}) collective-permute-start(bf16[256,1024]{1,0:T(8,128)(2,1)S(1)} %collective-permute-done.4.refs_4_), channel_id=1, source_target_pairs={{0,1},{1,0},{2,3},{3,2},{4,5},{5,4},{6,7},{7,6},{8,9},{9,8},{10,11... | collective-permute-start | bytes 1572872 | tf_op jit(solution)/shard_map/ppermute | solution.py:306
  91.2 3.2 %collective-permute-start.8 = (bf16[256,1024]{1,0:T(8,128)(2,1)S(1)}, bf16[256,1024]{1,0:T(8,128)(2,1)S(1)}, u32[]{:S(2)}, u32[]{:S(2)}) collective-permute-start(bf16[256,1024]{1,0:T(8,128)(2,1)S(1)} %constant_dynamic-update-slice_fusion.refs_6_), channel_id=1, source_target_pairs={{0,1},{1,0},{2,3},{3,2},{4,5},{5,4},{6,7},{7,6},{8,9},{9,8},{10,11... | collective-permute-start | bytes 1572872 | tf_op jit(solution)/shard_map/ppermute | solution.py:306
  94.4 1.9 %collective-permute-start.1 = (bf16[256,1024]{1,0:T(8,128)(2,1)S(1)}, bf16[256,1024]{1,0:T(8,128)(2,1)S(1)}, u32[]{:S(2)}, u32[]{:S(2)}) collective-permute-start(bf16[256,1024]{1,0:T(8,128)(2,1)S(1)} %all_gather.3.refs_0_), channel_id=1, source_target_pairs={{0,1},{1,0},{2,3},{3,2},{4,5},{5,4},{6,7},{7,6},{8,9},{9,8},{10,11... | collective-permute-start | bytes 1572872 | tf_op jit(solution)/shard_map/ppermute | solution.py:306
  97.1 6.2 %collective-permute-done.near_ref = bf16[8,32,2048]{2,1,0:T(8,128)(2,1)S(1)} collective-permute-done((bf16[8,32,2048]{2,1,0:T(8,128)(2,1)S(1)}, bf16[8,32,2048]{2,1,0:T(8,128)(2,1)S(1)}, u32[]{:S(2)}, u32[]{:S(2)}) %collective-permute-start) | collective-permute-done | bytes 1048608 | tf_op jit(solution)/shard_map/ppermute | solution.py:300
  103.4 3.7 %shard_map.65 = (bf16[512,1024]{1,0:T(8,128)(2,1)S(1)}, f32[16,2,128]{2,1,0:T(2,128)}) custom-call(bf16[512,2048]{1,0:T(8,128)(2,1)S(1)} %bitcast.4, f32[48,1024]{1,0:T(8,128)S(1)} %shard_map.64.levels_ref, bf16[256,1024]{1,0:T(8,128)(2,1)S(1)} %all_gather.3.refs_0_, bf16[256,1024]{1,0:T(8,128)(2,1)S(1)} %collective-permute-done.1.refs_1_, ...), custom_call_target="tpu_custom_call" | custom-call | tf_op jit(solution)/shard_map/pallas_call | solution.py:244
  107.2 1.0 copy-done.4
  108.2 4.6 %all-to-all-start.3 = ((f32[16,2,128]{2,1,0:T(2,128)}), f32[16,2,128]{2,1,0:T(2,128)S(1)}, u32[]{:S(2)}, u32[]{:S(2)}) async-start(f32[16,2,128]{2,1,0:T(2,128)} %get-tuple-element.20), calls=%async_computation.3 | async-start | bytes 32768 | tf_op jit(solution)/shard_map/all_to_all | solution.py:319
  112.8 3.3 %shard_map.66 = bf16[512,1024]{1,0:T(8,128)(2,1)} custom-call(bf16[512,1024]{1,0:T(8,128)(2,1)} %copy-done.4), custom_call_target="tpu_custom_call" | custom-call | flops 1073741824 | bytes 2097152 | tf_op jit(solution)/shard_map/pallas_call | solution.py:244
  116.1 4.0 %all-to-all-done.3.in_ref = f32[16,2,128]{2,1,0:T(2,128)S(1)} async-done(((f32[16,2,128]{2,1,0:T(2,128)}), f32[16,2,128]{2,1,0:T(2,128)S(1)}, u32[]{:S(2)}, u32[]{:S(2)}) %all-to-all-start.3) | async-done | bytes 16416 | tf_op jit(solution)/shard_map/all_to_all | solution.py:319
  120.1 11.7 %all_to_all.27.in_ref = f32[32,2,128]{2,1,0:T(2,128)S(1)} all-to-all(f32[32,2,128]{2,1,0:T(2,128)S(1)} %shard_map.67), channel_id=1, replica_groups=mesh['y'=8,'zl'=2,'x'=4,'zh'=4,'k'=2] {'y','x'}, dimensions={0} | all-to-all | bytes 65536 | tf_op jit(solution)/shard_map/all_to_all | solution.py:322
  131.8 0.8 shard_map.68
  (26 shorter events, 1.3 us)
Async XLA Ops:
  0.6 0.9 copy-start
  44.4 51.9 %copy-start.1 = (f32[1024]{0:T(1024)S(1)}, f32[1024]{0:T(1024)}, u32[]{:S(2)}) copy-start(f32[1024]{0:T(1024)} %param.6) | copy-start | bytes 12292
  44.4 52.0 %copy-start.2 = (f32[16]{0:T(128)S(1)}, f32[16]{0:T(128)}, u32[]{:S(2)}) copy-start(f32[16]{0:T(128)} %occ_ref.1) | copy-start | bytes 196
  44.4 52.0 %copy-start.3 = (s32[16]{0:T(128)S(1)}, s32[16]{0:T(128)}, u32[]{:S(2)}) copy-start(s32[16]{0:T(128)} %slot_ref.1) | copy-start | bytes 196
  44.4 32.8 %all-to-all-start.2 = ((bf16[8,32,2048]{2,1,0:T(8,128)(2,1)}), bf16[8,32,2048]{2,1,0:T(8,128)(2,1)S(1)}, u32[]{:S(2)}, u32[]{:S(2)}) async-start(bf16[8,32,2048]{2,1,0:T(8,128)(2,1)} %shard_map.60), calls=%async_computation.2 | async-start | bytes 2097152 | tf_op jit(solution)/shard_map/all_to_all | solution.py:297
  61.8 17.6 %collective-permute-start.2 = (bf16[256,1024]{1,0:T(8,128)(2,1)S(1)}, bf16[256,1024]{1,0:T(8,128)(2,1)S(1)}, u32[]{:S(2)}, u32[]{:S(2)}) collective-permute-start(bf16[256,1024]{1,0:T(8,128)(2,1)S(1)} %all_gather.3.refs_0_), channel_id=1, source_target_pairs={{0,8},{8,16},{16,24},{24,0},{1,9},{9,17},{17,25},{25,1},{2,10},{10... | collective-permute-start | bytes 1572872 | tf_op jit(solution)/shard_map/ppermute | solution.py:302
  64.2 17.5 %collective-permute-start.4 = (bf16[256,1024]{1,0:T(8,128)(2,1)S(1)}, bf16[256,1024]{1,0:T(8,128)(2,1)S(1)}, u32[]{:S(2)}, u32[]{:S(2)}) collective-permute-start(bf16[256,1024]{1,0:T(8,128)(2,1)S(1)} %all_gather.3.refs_0_), channel_id=1, source_target_pairs={{0,24},{8,0},{16,8},{24,16},{1,25},{9,1},{17,9},{25,17},{2,26},{10... | collective-permute-start | bytes 1572872 | tf_op jit(solution)/shard_map/ppermute | solution.py:302
  77.2 26.1 %collective-permute-start = (bf16[8,32,2048]{2,1,0:T(8,128)(2,1)S(1)}, bf16[8,32,2048]{2,1,0:T(8,128)(2,1)S(1)}, u32[]{:S(2)}, u32[]{:S(2)}) collective-permute-start(bf16[8,32,2048]{2,1,0:T(8,128)(2,1)S(1)} %all-to-all-done.2.own_ref), channel_id=1, source_target_pairs={{0,32},{32,0},{1,33},{33,1},{2,34},{34,2},{3,35},{35,3},{4,36},{36... | collective-permute-start | bytes 3145736 | tf_op jit(solution)/shard_map/ppermute | solution.py:300
  79.4 11.7 %collective-permute-start.6 = (bf16[128,1024]{1,0:T(8,128)(2,1)S(1)}, bf16[128,1024]{1,0:T(8,128)(2,1)S(1)}, u32[]{:S(2)}, u32[]{:S(2)}) collective-permute-start(bf16[128,1024]{1,0:T(8,128)(2,1)S(1)} %slice.8), channel_id=1, source_target_pairs={{0,8},{8,16},{16,24},{24,0},{1,9},{9,17},{17,25},{25,1},{2,10},{10... | collective-permute-start | bytes 786440 | tf_op jit(solution)/shard_map/ppermute | solution.py:304
  81.7 9.5 %collective-permute-start.7 = (bf16[128,1024]{1,0:T(8,128)(2,1)S(1)}, bf16[128,1024]{1,0:T(8,128)(2,1)S(1)}, u32[]{:S(2)}, u32[]{:S(2)}) collective-permute-start(bf16[128,1024]{1,0:T(8,128)(2,1)S(1)} %slice.9), channel_id=1, source_target_pairs={{0,24},{8,0},{16,8},{24,16},{1,25},{9,1},{17,9},{25,17},{2,26},{10... | collective-permute-start | bytes 786440 | tf_op jit(solution)/shard_map/ppermute | solution.py:304
  86.0 17.4 %collective-permute-start.3 = (bf16[256,1024]{1,0:T(8,128)(2,1)S(1)}, bf16[256,1024]{1,0:T(8,128)(2,1)S(1)}, u32[]{:S(2)}, u32[]{:S(2)}) collective-permute-start(bf16[256,1024]{1,0:T(8,128)(2,1)S(1)} %collective-permute-done.2.refs_2_), channel_id=1, source_target_pairs={{0,1},{1,0},{2,3},{3,2},{4,5},{5,4},{6,7},{7,6},{8,9},{9,8},{10,11... | collective-permute-start | bytes 1572872 | tf_op jit(solution)/shard_map/ppermute | solution.py:306
  89.2 14.2 %collective-permute-start.5 = (bf16[256,1024]{1,0:T(8,128)(2,1)S(1)}, bf16[256,1024]{1,0:T(8,128)(2,1)S(1)}, u32[]{:S(2)}, u32[]{:S(2)}) collective-permute-start(bf16[256,1024]{1,0:T(8,128)(2,1)S(1)} %collective-permute-done.4.refs_4_), channel_id=1, source_target_pairs={{0,1},{1,0},{2,3},{3,2},{4,5},{5,4},{6,7},{7,6},{8,9},{9,8},{10,11... | collective-permute-start | bytes 1572872 | tf_op jit(solution)/shard_map/ppermute | solution.py:306
  91.2 12.2 %collective-permute-start.8 = (bf16[256,1024]{1,0:T(8,128)(2,1)S(1)}, bf16[256,1024]{1,0:T(8,128)(2,1)S(1)}, u32[]{:S(2)}, u32[]{:S(2)}) collective-permute-start(bf16[256,1024]{1,0:T(8,128)(2,1)S(1)} %constant_dynamic-update-slice_fusion.refs_6_), channel_id=1, source_target_pairs={{0,1},{1,0},{2,3},{3,2},{4,5},{5,4},{6,7},{7,6},{8,9},{9,8},{10,11... | collective-permute-start | bytes 1572872 | tf_op jit(solution)/shard_map/ppermute | solution.py:306
  94.4 9.0 %collective-permute-start.1 = (bf16[256,1024]{1,0:T(8,128)(2,1)S(1)}, bf16[256,1024]{1,0:T(8,128)(2,1)S(1)}, u32[]{:S(2)}, u32[]{:S(2)}) collective-permute-start(bf16[256,1024]{1,0:T(8,128)(2,1)S(1)} %all_gather.3.refs_0_), channel_id=1, source_target_pairs={{0,1},{1,0},{2,3},{3,2},{4,5},{5,4},{6,7},{7,6},{8,9},{9,8},{10,11... | collective-permute-start | bytes 1572872 | tf_op jit(solution)/shard_map/ppermute | solution.py:306
  107.2 1.0 copy-start.4
  108.2 12.0 %all-to-all-start.3 = ((f32[16,2,128]{2,1,0:T(2,128)}), f32[16,2,128]{2,1,0:T(2,128)S(1)}, u32[]{:S(2)}, u32[]{:S(2)}) async-start(f32[16,2,128]{2,1,0:T(2,128)} %get-tuple-element.20), calls=%async_computation.3 | async-start | bytes 32768 | tf_op jit(solution)/shard_map/all_to_all | solution.py:319
